TPU v7x, 32 devices: a whole 2x2x4 slice. The times are simulated.
32 devices in a mesh: dp: 16 (over z, x, core), tensor: 2 (over y).
Axes of the slice: x: 2, y: 2, z: 4, core: 2. Of those that a mesh axis runs over, the one named last changes fastest.
Arguments:
- tokens: bfloat16 [32768, 1024], P(('dp', 'tensor')), may hold values from -6 to 6
- first_gain: float32 [1024], replicated, may hold values from 0.1 to 1.9
- first_bias: float32 [1024], replicated, may hold values from -3 to 3
- qkv_weight: bfloat16 [1024, 3, 1024], P(None, None, 'tensor'), may hold values from -0.1875 to 0.1875
- qv_bias: float32 [2, 1024], P(None, 'tensor'), may hold values from -3 to 3
- out_weight: bfloat16 [1024, 1024], P('tensor'), may hold values from -1.5 to 1.5
- out_bias: float32 [1024], replicated, may hold values from -3 to 3
- attention_scale: float32 [1024], replicated, may hold values from 0.5 to 2
- second_gain: float32 [1024], replicated, may hold values from 0.1 to 1.9
- second_bias: float32 [1024], replicated, may hold values from -3 to 3
- up_weight: bfloat16 [1024, 4096], P(None, 'tensor'), may hold values from -0.1875 to 0.1875
- up_bias: float32 [4096], P('tensor'), may hold values from -3 to 3
- down_weight: bfloat16 [4096, 1024], P('tensor'), may hold values from -0.09375 to 0.09375
- down_bias: float32 [1024], replicated, may hold values from -3 to 3
- mlp_scale: float32 [1024], replicated, may hold values from 0.5 to 2
- cotangent: bfloat16 [32768, 1024], P(('dp', 'tensor')), may hold values from -6 to 6
Outputs:
- block_out: bfloat16 [32768, 1024], P(('dp', 'tensor'))
- input_grad: float32 [32768, 1024], P(('dp', 'tensor'))
- first_gain_grad: float32 [1024], replicated
- first_bias_grad: float32 [1024], replicated
- qkv_weight_grad: float32 [1024, 3, 1024], P(None, None, 'tensor')
- qv_bias_grad: float32 [2, 1024], P(None, 'tensor')
- out_weight_grad: float32 [1024, 1024], P('tensor')
- out_bias_grad: float32 [1024], replicated
- attention_scale_grad: float32 [1024], replicated
- second_gain_grad: float32 [1024], replicated
- second_bias_grad: float32 [1024], replicated
- up_weight_grad: float32 [1024, 4096], P(None, 'tensor')
- up_bias_grad: float32 [4096], P('tensor')
- down_weight_grad: float32 [4096, 1024], P('tensor')
- down_bias_grad: float32 [1024], replicated
- mlp_scale_grad: float32 [1024], replicated
All inputs are finite; a program needn't handle non-finite values.
Results may differ from a plain program's by a relative error of at most 0.019.
Values may be sent and summed in bfloat16 or wider, within the bound.
A program may use at most 256 MiB of HBM per device.

v0:
```python
import jax
import jax.numpy as jnp
from jax import lax
from jax.sharding import PartitionSpec as P

HD = 64
SEQ = 1024


EPSILON = 1e-06


def norm_rows(values, gain, shift):
    center = values - jnp.mean(values, axis=-1, keepdims=True)
    spread = jnp.mean(center * center, axis=-1, keepdims=True)
    return center * lax.rsqrt(spread + EPSILON) * gain + shift


def exact_gelu(values):
    return jax.nn.gelu(values, approximate=False)


def attend_forward(query, keys, values):
    factor = query.shape[-1] ** (-0.5)
    scores = jnp.einsum("qhd,khd->hqk", query, keys, preferred_element_type=jnp.float32) * factor
    row_peak = jnp.max(scores, axis=-1, keepdims=True)
    powers = jnp.exp(scores - row_peak)
    totals = jnp.sum(powers, axis=-1, keepdims=True)
    probs = (powers / totals).astype(jnp.bfloat16)
    mixed = jnp.einsum("hqk,khd->qhd", probs, values, preferred_element_type=jnp.float32).astype(
        jnp.bfloat16
    )
    return (mixed, row_peak[..., 0] + jnp.log(totals[..., 0]))


def attend_backward(carry, piece, keys, values):
    query, grad_out, log_totals = piece
    factor = query.shape[-1] ** (-0.5)
    scores = jnp.einsum("qhd,khd->hqk", query, keys, preferred_element_type=jnp.float32) * factor
    probs = jnp.exp(scores - log_totals[..., None])
    low_probs = probs.astype(jnp.bfloat16)
    grad_values = carry[1] + jnp.einsum(
        "hqk,qhd->khd", low_probs, grad_out, preferred_element_type=jnp.float32
    )
    grad_probs = jnp.einsum("qhd,khd->hqk", grad_out, values, preferred_element_type=jnp.float32)
    delta = jnp.sum(grad_probs * probs, axis=-1, keepdims=True)
    grad_scores = (probs * (grad_probs - delta)).astype(jnp.bfloat16)
    grad_query = (
        jnp.einsum("hqk,khd->qhd", grad_scores, keys, preferred_element_type=jnp.float32) * factor
    ).astype(jnp.bfloat16)
    grad_keys = (
        carry[0]
        + jnp.einsum("hqk,qhd->khd", grad_scores, query, preferred_element_type=jnp.float32)
        * factor
    )
    return ((grad_keys, grad_values), grad_query)


def body(
    tokens,
    first_gain,
    first_bias,
    qkv_weight,
    qv_bias,
    out_weight,
    out_bias,
    attention_scale,
    second_gain,
    second_bias,
    up_weight,
    up_bias,
    down_weight,
    down_bias,
    mlp_scale,
    cotangent,
):
    local_rows, width = tokens.shape
    group_size = lax.axis_size("tensor")
    total_rows = local_rows * group_size
    columns = qkv_weight.shape[2]
    heads_here = columns // HD
    block = min(512, SEQ)
    block_count = SEQ // block
    images = total_rows // SEQ
    image_shape = (images, SEQ, heads_here, HD)
    qkv_flat = qkv_weight.reshape(width, 3 * columns)
    residual = tokens.astype(jnp.float32)
    first_norm = norm_rows(residual, first_gain, first_bias).astype(jnp.bfloat16)
    normed = lax.all_gather(first_norm, "tensor", axis=0, tiled=True)
    projected = jnp.dot(normed, qkv_flat, preferred_element_type=jnp.float32)
    query = (projected[:, :columns] + qv_bias[0]).astype(jnp.bfloat16)
    keys = projected[:, columns : 2 * columns].astype(jnp.bfloat16)
    values = (projected[:, 2 * columns :] + qv_bias[1]).astype(jnp.bfloat16)

    def forward_image(parts):
        image_query, image_keys, image_values = parts
        blocks = image_query.reshape(block_count, block, heads_here, HD)
        mixed_blocks, log_blocks = lax.map(
            lambda piece: attend_forward(piece, image_keys, image_values), blocks
        )
        return (mixed_blocks.reshape(SEQ, heads_here, HD), log_blocks)

    mixed, log_totals = lax.map(
        forward_image,
        (query.reshape(image_shape), keys.reshape(image_shape), values.reshape(image_shape)),
    )
    mixed = mixed.reshape(total_rows, columns)
    attention = (
        lax.psum_scatter(
            jnp.dot(mixed, out_weight, preferred_element_type=jnp.float32),
            "tensor",
            scatter_dimension=0,
            tiled=True,
        )
        + out_bias
    )
    after_attention = residual + attention_scale * attention
    second_norm = norm_rows(after_attention, second_gain, second_bias).astype(jnp.bfloat16)
    normed_second = lax.all_gather(second_norm, "tensor", axis=0, tiled=True)
    pre_act = jnp.dot(normed_second, up_weight, preferred_element_type=jnp.float32) + up_bias
    activated, gelu_pull = jax.vjp(exact_gelu, pre_act)
    hidden = activated.astype(jnp.bfloat16)
    feed = (
        lax.psum_scatter(
            jnp.dot(hidden, down_weight, preferred_element_type=jnp.float32).astype(jnp.bfloat16),
            "tensor",
            scatter_dimension=0,
            tiled=True,
        ).astype(jnp.float32)
        + down_bias
    )
    block_out = (after_attention + mlp_scale * feed).astype(jnp.bfloat16)
    upstream = cotangent.astype(jnp.float32)
    grad_mlp_scale = jnp.sum(upstream * feed, axis=0)
    grad_feed = (upstream * mlp_scale).astype(jnp.bfloat16)
    grad_down_bias = jnp.sum(grad_feed.astype(jnp.float32), axis=0)
    feed_rows = lax.all_gather(grad_feed, "tensor", axis=0, tiled=True)
    grad_down_weight = jnp.dot(hidden.T, feed_rows, preferred_element_type=jnp.float32)
    grad_hidden = jnp.dot(feed_rows, down_weight.T, preferred_element_type=jnp.float32)
    grad_pre = gelu_pull(grad_hidden)[0].astype(jnp.bfloat16)
    grad_up_bias = jnp.sum(grad_pre.astype(jnp.float32), axis=0)
    grad_up_weight = jnp.dot(normed_second.T, grad_pre, preferred_element_type=jnp.float32)
    grad_second = lax.psum_scatter(
        jnp.dot(grad_pre, up_weight.T, preferred_element_type=jnp.float32),
        "tensor",
        scatter_dimension=0,
        tiled=True,
    )
    second_value, second_pull = jax.vjp(norm_rows, after_attention, second_gain, second_bias)
    grad_after, grad_second_gain, grad_second_bias = second_pull(grad_second)
    grad_after = grad_after + upstream
    grad_attention_scale = jnp.sum(grad_after * attention, axis=0)
    grad_attention = (grad_after * attention_scale).astype(jnp.bfloat16)
    grad_out_bias = jnp.sum(grad_attention.astype(jnp.float32), axis=0)
    attention_rows = lax.all_gather(grad_attention, "tensor", axis=0, tiled=True)
    grad_out_weight = jnp.dot(mixed.T, attention_rows, preferred_element_type=jnp.float32)
    grad_mixed = jnp.dot(attention_rows, out_weight.T, preferred_element_type=jnp.float32).astype(
        jnp.bfloat16
    )

    def backward_image(parts):
        image_query, image_keys, image_values, image_grad, image_logs = parts
        blocks = (
            image_query.reshape(block_count, block, heads_here, HD),
            image_grad.reshape(block_count, block, heads_here, HD),
            image_logs,
        )
        zeros = jnp.zeros((SEQ, heads_here, HD), jnp.float32)
        sums, grad_query_blocks = lax.scan(
            lambda carry, piece: attend_backward(carry, piece, image_keys, image_values),
            (zeros, zeros),
            blocks,
        )
        return (
            grad_query_blocks.reshape(SEQ, heads_here, HD),
            sums[0].astype(jnp.bfloat16),
            sums[1].astype(jnp.bfloat16),
        )

    grad_query, grad_keys, grad_values = lax.map(
        backward_image,
        (
            query.reshape(image_shape),
            keys.reshape(image_shape),
            values.reshape(image_shape),
            grad_mixed.reshape(image_shape),
            log_totals,
        ),
    )
    grad_query = grad_query.reshape(total_rows, columns)
    grad_keys = grad_keys.reshape(total_rows, columns)
    grad_values = grad_values.reshape(total_rows, columns)
    grad_qv_bias = jnp.stack(
        [
            jnp.sum(grad_query.astype(jnp.float32), axis=0),
            jnp.sum(grad_values.astype(jnp.float32), axis=0),
        ]
    )
    grad_projected = jnp.concatenate([grad_query, grad_keys, grad_values], axis=1)
    grad_qkv_weight = jnp.dot(normed.T, grad_projected, preferred_element_type=jnp.float32).reshape(
        width, 3, columns
    )
    grad_first = lax.psum_scatter(
        jnp.dot(grad_projected, qkv_flat.T, preferred_element_type=jnp.float32).astype(
            jnp.bfloat16
        ),
        "tensor",
        scatter_dimension=0,
        tiled=True,
    ).astype(jnp.float32)
    first_value, first_pull = jax.vjp(norm_rows, residual, first_gain, first_bias)
    grad_input, grad_first_gain, grad_first_bias = first_pull(grad_first)
    grad_input = grad_input + grad_after
    weights = (
        lax.psum(grad_qkv_weight.astype(jnp.bfloat16), "dp").astype(jnp.float32),
        lax.psum(grad_qv_bias.astype(jnp.bfloat16), "dp").astype(jnp.float32),
        lax.psum(grad_out_weight.astype(jnp.bfloat16), "dp").astype(jnp.float32),
        lax.psum(grad_up_weight.astype(jnp.bfloat16), "dp").astype(jnp.float32),
        lax.psum(grad_up_bias.astype(jnp.bfloat16), "dp").astype(jnp.float32),
        lax.psum(grad_down_weight.astype(jnp.bfloat16), "dp").astype(jnp.float32),
    )
    shared = lax.psum(
        (
            grad_first_gain,
            grad_first_bias,
            grad_out_bias,
            grad_attention_scale,
            grad_second_gain,
            grad_second_bias,
            grad_down_bias,
            grad_mlp_scale,
        ),
        ("dp", "tensor"),
    )
    return (
        block_out,
        grad_input,
        shared[0],
        shared[1],
        weights[0],
        weights[1],
        weights[2],
        shared[2],
        shared[3],
        shared[4],
        shared[5],
        weights[3],
        weights[4],
        weights[5],
        shared[6],
        shared[7],
    )


def solution(mesh):
    return jax.shard_map(
        body,
        mesh=mesh,
        in_specs=(
            P(("dp", "tensor"), None),
            P(),
            P(),
            P(None, None, "tensor"),
            P(None, "tensor"),
            P("tensor", None),
            P(),
            P(),
            P(),
            P(),
            P(None, "tensor"),
            P("tensor"),
            P("tensor", None),
            P(),
            P(),
            P(("dp", "tensor"), None),
        ),
        out_specs=(
            P(("dp", "tensor"), None),
            P(("dp", "tensor"), None),
            P(),
            P(),
            P(None, None, "tensor"),
            P(None, "tensor"),
            P("tensor", None),
            P(),
            P(),
            P(),
            P(),
            P(None, "tensor"),
            P("tensor"),
            P("tensor", None),
            P(),
            P(),
        ),
        check_vma=False,
    )
```

profile of v0, /device:TPU:1, one launch (start us, length us, event | category | flops | bytes accessed | tf_op | source)
XLA Modules:
  0.0 1289.4 jit_solution(17048986658993472038)
XLA Ops:
  19.8 54.2 %all-gather.5.cloned.1.call-done = bf16[2048,1024]{1,0:T(8,128)(2,1)} async-done(((bf16[1024,1024]{1,0:T(8,128)(2,1)}), bf16[2048,1024]{1,0:T(8,128)(2,1)}) %all-gather.5.cloned.1.call-update) | async-done | bytes 4194320 | tf_op jit(solution)/shard_map/all_gather | solution.py:89
  74.0 9.5 fusion.67
  87.0 6.1 reshape.188
  93.1 5.5 copy.52
  102.2 5.6 copy.51
  119.4 63.9 %while.54 = (s32[]{:T(128)}, bf16[2,1024,8,64]{3,2,1,0:T(8,128)(2,1)}, f32[2,2,8,512]{3,2,1,0:T(8,128)}, bf16[2,1024,8,64]{1,3,2,0:T(8,128)(2,1)}, bf16[2,1024,8...) while((s32[]{:T(128)}, ...), condition=%wide.region_7.8_spmd, body=%wide.region_2.7_spmd.sunk | while | flops 1111748608 | bytes 82510232 | solution.py:103
  124.7 22.6 %while.57 = (s32[]{:T(128)}, bf16[2,512,8,64]{1,3,2,0:T(8,128)(2,1)}, f32[2,8,512]{2,1,0:T(8,128)S(1)}, bf16[2,512,8,64]{1,3,2,0:T(8,128)(2,1)S(1)}, bf16[1024,8...) while((s32[]{:T(128)}, bf16[2,512,8,64]{1,3,2,0:T(8,128)(2,1)}, ...), condition=%wide.region_6.6_spmd, body=%wide.region_3.5_spmd.sunk | while | flops 1111748608 | bytes 66191540 | solution.py:98
  156.6 22.6 %while.57 = (s32[]{:T(128)}, bf16[2,512,8,64]{1,3,2,0:T(8,128)(2,1)}, f32[2,8,512]{2,1,0:T(8,128)S(1)}, bf16[2,512,8,64]{1,3,2,0:T(8,128)(2,1)S(1)}, bf16[1024,8...) while((s32[]{:T(128)}, bf16[2,512,8,64]{1,3,2,0:T(8,128)(2,1)}, ...), condition=%wide.region_6.6_spmd, body=%wide.region_3.5_spmd.sunk | while | flops 1111748608 | bytes 66191540 | solution.py:98
  188.7 5.7 fusion.68
  194.5 99.3 %reduce-scatter.5.cloned.1.call-done = f32[1024,1024]{1,0:T(8,128)} async-done(((f32[2048,1024]{1,0:T(8,128)}), f32[1024,1024]{1,0:T(8,128)}) %reduce-scatter.5.cloned.1.call-update) | async-done | bytes 4194320 | tf_op jit(solution)/shard_map/reduce_scatter | solution.py:109
  304.3 54.1 %all-gather.7.cloned.1.call-done = bf16[2048,1024]{1,0:T(8,128)(2,1)} async-done(((bf16[1024,1024]{1,0:T(8,128)(2,1)}), bf16[2048,1024]{1,0:T(8,128)(2,1)}) %all-gather.7.cloned.1.call-update) | async-done | bytes 4194320 | tf_op jit(solution)/shard_map/all_gather | solution.py:119
  358.5 49.6 %multiply_convert_fusion.1 = (bf16[2048,2048]{1,0:T(8,128)(2,1)}, f32[2048,2048]{1,0:T(8,128)}, f32[2048,2048]{1,0:T(8,128)}) fusion(f32[2048]{0:T(1024)S(1)} %copy-done.69, bf16[2048,1024]{1,0:T(8,128)(2,1)} %all-gather.7.cloned.1.call-done, bf16[1024,2048]{1,0:T(8,128)(2,1)} %param.34), kind=kOutput, calls=%fused_computation.59 | convolution fusion | flops 8866758656 | bytes 50339840 | tf_op jit(solution)/shard_map/dot_general | solution.py:120
  408.1 9.2 all-gather.9.cloned.1.call-done
  417.3 23.6 %fusion.66 = (bf16[2048]{0:T(1024)(128)(2,1)}, bf16[2048,2048]{1,0:T(8,128)(2,1)}) fusion(f32[2048,2048]{1,0:T(8,128)} %get-tuple-element.366, bf16[2048,1024]{1,0:T(8,128)(2,1)} %all-gather.9.cloned.1.call-done, bf16[2048,1024]{1,0:T(8,128)(2,1)} %param.36, f32[2048,2048]{1,0:T(8,128)} %get-tuple-element.383, f32[2048]{0:T(1024)S(1)} %copy-done.69), kind=kOutput, calls=%fused_computation.138 | convolution fusion | flops 8657041408 | bytes 50343936 | tf_op jit(solution)/shard_map/dot_general | solution.py:139
  440.9 13.4 %fusion.69 = f32[2048,1024]{1,0:T(8,128)} fusion(bf16[2048,2048]{1,0:T(8,128)(2,1)} %get-tuple-element.385, bf16[1024,2048]{1,0:T(8,128)(2,1)S(1)} %copy-done.67), kind=kOutput, calls=%fused_computation.141 | convolution fusion | flops 8589934592 | bytes 20971520 | tf_op jit(solution)/shard_map/dot_general | solution.py:144
  454.4 13.8 %convolution_convert_fusion.3 = bf16[2048,1024]{1,0:T(8,128)(2,1)} fusion(bf16[2048,2048]{1,0:T(8,128)(2,1)} %get-tuple-element.365, bf16[2048,1024]{1,0:T(8,128)(2,1)} %param.36), kind=kOutput, calls=%fused_computation.117 | convolution fusion | flops 8592031744 | bytes 16777216 | tf_op jit(solution)/shard_map/dot_general | solution.py:125
  468.3 85.4 %reduce-scatter.9.cloned.1.call-done = f32[1024,1024]{1,0:T(8,128)} async-done(((f32[2048,1024]{1,0:T(8,128)}), f32[1024,1024]{1,0:T(8,128)}) %reduce-scatter.9.cloned.1.call-update) | async-done | bytes 4194320 | tf_op jit(solution)/shard_map/reduce_scatter | solution.py:143
  558.7 52.1 %reduce-scatter.7.cloned.1.call-done = bf16[1024,1024]{1,0:T(8,128)(2,1)} async-done(((bf16[2048,1024]{1,0:T(8,128)(2,1)}), bf16[1024,1024]{1,0:T(8,128)(2,1)}) %reduce-scatter.7.cloned.1.call-update) | async-done | bytes 2097168 | tf_op jit(solution)/shard_map/reduce_scatter | solution.py:124
  610.8 6.0 fusion.62
  620.2 14.3 %convolution_convert_fusion.4 = bf16[2048,1024]{1,0:T(8,128)(2,1)} fusion(bf16[2048,2048]{1,0:T(8,128)(2,1)} %get-tuple-element.365, bf16[2048,1024]{1,0:T(8,128)(2,1)} %all-gather.9.cloned.1.call-done), kind=kOutput, calls=%fused_computation.118 | convolution fusion | flops 8592031744 | bytes 16777216 | tf_op jit(solution)/shard_map/dot_general | solution.py:138
  634.5 13.1 %convolution_convert_fusion.2 = bf16[1024,2048]{1,0:T(8,128)(2,1)} fusion(bf16[2048,1024]{1,0:T(8,128)(2,1)S(1)} %copy-done.68, bf16[2048,2048]{1,0:T(8,128)(2,1)} %get-tuple-element.385), kind=kOutput, calls=%fused_computation.116 | convolution fusion | flops 8592031744 | bytes 16777216 | tf_op jit(solution)/shard_map/dot_general | solution.py:142
  647.6 29.4 %all-gather.11.cloned.1.call-done = bf16[2048,1024]{1,0:T(8,128)(2,1)} async-done(((bf16[1024,1024]{1,0:T(8,128)(2,1)}), bf16[2048,1024]{1,0:T(8,128)(2,1)}) %all-gather.11.cloned.1.call-update) | async-done | bytes 4194320 | tf_op jit(solution)/shard_map/all_gather | solution.py:155
  693.2 202.7 %while.56 = (s32[]{:T(128)}, bf16[2,1024,8,64]{3,2,1,0:T(8,128)(2,1)}, bf16[2,1024,8,64]{1,3,2,0:T(8,128)(2,1)}, bf16[2,1024,8,64]{1,3,2,0:T(8,128)(2,1)}, bf16[...) while((s32[]{:T(128)}, ...), condition=%wide.region_19.20_spmd, body=%wide.region_15.19_spmd.sunk | while | flops 2738876416 | bytes 270189184 | solution.py:180
  703.5 80.4 %while.58 = (s32[]{:T(128)}, f32[1024,8,64]{0,2,1:T(8,128)}, f32[1024,8,64]{0,2,1:T(8,128)}, bf16[2,512,8,64]{1,3,2,0:T(8,128)(2,1)}, bf16[2,512,8,64]{1,3,2,0:T...) while((s32[]{:T(128)}, f32[1024,8,64]{0,2,1:T(8,128)}, ...), condition=%wide.region_18.18_spmd.clone, body=%wide.region_16.17_spmd.clone.sunk | while | flops 2737827840 | bytes 190431472 | solution.py:169
  712.3 9.7 multiply_reduce_fusion.8
  721.9 10.4 multiply_convert_fusion.5
  732.4 7.0 fusion.124
  746.9 5.7 bitcast_add_fusion.5
  752.6 9.7 multiply_reduce_fusion.8
  762.3 10.4 multiply_convert_fusion.5
  772.7 7.0 fusion.124
  804.5 80.3 %while.58 = (s32[]{:T(128)}, f32[1024,8,64]{0,2,1:T(8,128)}, f32[1024,8,64]{0,2,1:T(8,128)}, bf16[2,512,8,64]{1,3,2,0:T(8,128)(2,1)}, bf16[2,512,8,64]{1,3,2,0:T...) while((s32[]{:T(128)}, f32[1024,8,64]{0,2,1:T(8,128)}, ...), condition=%wide.region_18.18_spmd.clone, body=%wide.region_16.17_spmd.clone.sunk | while | flops 2737827840 | bytes 190431472 | solution.py:169
  813.3 9.7 multiply_reduce_fusion.8
  823.0 10.4 multiply_convert_fusion.5
  833.4 7.0 fusion.124
  847.9 5.7 bitcast_add_fusion.5
  853.7 9.7 multiply_reduce_fusion.8
  863.3 10.4 multiply_convert_fusion.5
  873.7 7.0 fusion.124
  913.7 12.4 convolution_convert_fusion
  930.9 5.5 convolution_convert_fusion.6
  938.0 11.1 convolution_convert_fusion.1
  955.7 32.4 %all-reduce.1 = (bf16[2,512]{1,0:T(2,128)(2,1)S(1)}, bf16[2048]{0:T(1024)(128)(2,1)S(1)}) all-reduce(bf16[2,512]{1,0:T(2,128)(2,1)S(1)} %pad_maximum_fusion.3, bf16[2048]{0:T(1024)(128)(2,1)S(1)} %copy-done.64), channel_id=1, replica_groups=mesh['dp'=16,'tensor'=2] {'dp'}, use_global_device_ids=true, to_apply=%region_30.31 | all-reduce | flops 3072 | bytes 12288 | tf_op jit(solution)/shard_map/psum | solution.py:216
  989.2 182.1 %all-reduce.5.cloned.1.call-done = (bf16[1024,3,512]{0,2,1:T(8,128)(2,1)}, bf16[512,1024]{1,0:T(8,128)(2,1)}, bf16[1024,2048]{1,0:T(8,128)(2,1)}, bf16[2048,1024]{1,0:T(8,128)(2,1)}) async-done(((bf16[1024,3,512]{0,2,1:T(8,128)(2,1)}, bf16[512,1024]{1,0:T(8,128)(2,1)}, bf16[1024,2048]{1,0:T(8,128)(2,1)}, bf16[2048,1024]{1,0:T(8,128)(2,1)}), (bf16[1024,3,512]{0,2,1:T(8,128)(2,1)}, ...) | async-done | bytes 12582928 | tf_op jit(solution)/shard_map/psum | solution.py:215
  1179.5 7.5 convert_element_type.152
  1191.5 37.1 %reduce-scatter.11.cloned.1.call-done = bf16[1024,1024]{1,0:T(8,128)(2,1)} async-done(((bf16[2048,1024]{1,0:T(8,128)(2,1)}), bf16[1024,1024]{1,0:T(8,128)(2,1)}) %reduce-scatter.11.cloned.1.call-update) | async-done | bytes 2097168 | tf_op jit(solution)/shard_map/reduce_scatter | solution.py:203
  1236.0 6.8 fusion.52
  1242.8 39.7 %all-reduce = (f32[1024]{0:T(1024)}, f32[1024]{0:T(1024)}, f32[1024]{0:T(1024)}, f32[1024]{0:T(1024)}, f32[1024]{0:T(1024)}, /*index=5*/f32[1024]{0:T(1024)}, f32[1024]{0:T(1024)}, f32[1024]{0:T(1024)}) all-reduce(f32[1024]{0:T(1024)S(1)} %get-tuple-element.278, ...), channel_id=1, replica_groups=mesh['dp'=16,'tensor'=2] {'dp','tensor'}, use_global_device_ids=true, to_apply=%region_24.25 | all-reduce | flops 8192 | bytes 65536 | tf_op jit(solution)/shard_map/psum | solution.py:222
  (340 shorter events, 268.7 us)
Async XLA Ops:
  7.2 181.5 %copy-start = (bf16[512,1024]{1,0:T(8,128)(2,1)S(1)}, bf16[512,1024]{1,0:T(8,128)(2,1)}, u32[]{:S(2)}) copy-start(bf16[512,1024]{1,0:T(8,128)(2,1)} %param.29) | copy-start | bytes 3145732
  7.2 66.8 %all-gather.5.cloned.1.call-start = ((), (), s32[]{:S(2)}) async-start(), calls=%async_computation.4 | async-start | bytes 6291456 | tf_op jit(solution)/shard_map/all_gather | solution.py:89
  15.0 278.9 %reduce-scatter.5.cloned.1.call-start = ((), (), s32[]{:S(2)}) async-start(), calls=%async_computation.5 | async-start | bytes 12582912 | tf_op jit(solution)/shard_map/reduce_scatter | solution.py:109
  124.7 22.6 %copy-start.31 = (f32[2,2,8,512]{3,2,1,0:T(8,128)S(1)}, f32[2,2,8,512]{3,2,1,0:T(8,128)}, u32[]{:S(2)}) copy-start(f32[2,2,8,512]{3,2,1,0:T(8,128)} %get-tuple-element.693) | copy-start | bytes 196612 | tf_op jit(solution)/shard_map/while
  156.6 22.6 %copy-start.31 = (f32[2,2,8,512]{3,2,1,0:T(8,128)S(1)}, f32[2,2,8,512]{3,2,1,0:T(8,128)}, u32[]{:S(2)}) copy-start(f32[2,2,8,512]{3,2,1,0:T(8,128)} %get-tuple-element.693) | copy-start | bytes 196612 | tf_op jit(solution)/shard_map/while
  194.5 99.4 %copy-start.8 = (bf16[1024,1024]{1,0:T(8,128)(2,1)S(1)}, bf16[1024,1024]{1,0:T(8,128)(2,1)}, u32[]{:S(2)}) copy-start(bf16[1024,1024]{1,0:T(8,128)(2,1)} %param.24) | copy-start | bytes 6291460
  194.5 99.4 %copy-start.53 = (f32[1024]{0:T(1024)S(1)}, f32[1024]{0:T(1024)}, u32[]{:S(2)}) copy-start(f32[1024]{0:T(1024)} %param.31) | copy-start | bytes 12292
  194.5 99.4 %copy-start.55 = (f32[1024]{0:T(1024)S(1)}, f32[1024]{0:T(1024)}, u32[]{:S(2)}) copy-start(f32[1024]{0:T(1024)} %param.30) | copy-start | bytes 12292
  194.5 164.0 %all-gather.7.cloned.1.call-start = ((), (), s32[]{:S(2)}) async-start(), calls=%async_computation.6 | async-start | bytes 6291456 | tf_op jit(solution)/shard_map/all_gather | solution.py:119
  301.5 56.9 %copy-start.69 = (f32[2048]{0:T(1024)S(1)}, f32[2048]{0:T(1024)}, u32[]{:S(2)}) copy-start(f32[2048]{0:T(1024)} %param.35) | copy-start | bytes 24580
  301.6 115.7 %all-gather.9.cloned.1.call-start = ((), (), s32[]{:S(2)}) async-start(), calls=%async_computation.8 | async-start | bytes 6291456 | tf_op jit(solution)/shard_map/all_gather | solution.py:137
  304.3 249.5 %reduce-scatter.9.cloned.1.call-start = ((), (), s32[]{:S(2)}) async-start(), calls=%async_computation.9 | async-start | bytes 12582912 | tf_op jit(solution)/shard_map/reduce_scatter | solution.py:143
  417.3 23.6 %copy-start.67 = (bf16[1024,2048]{1,0:T(8,128)(2,1)S(1)}, bf16[1024,2048]{1,0:T(8,128)(2,1)}, u32[]{:S(2)}) copy-start(bf16[1024,2048]{1,0:T(8,128)(2,1)} %param.34) | copy-start | bytes 12582916
  454.4 156.4 %reduce-scatter.7.cloned.1.call-start = ((), (), s32[]{:S(2)}) async-start(), calls=%async_computation.7 | async-start | bytes 6291456 | tf_op jit(solution)/shard_map/reduce_scatter | solution.py:124
  468.2 85.6 %copy-start.36 = (f32[1024]{0:T(1024)S(1)}, f32[1024]{0:T(1024)}, u32[]{:S(2)}) copy-start(f32[1024]{0:T(1024)} %copy-done.35) | copy-start | bytes 12292
  468.2 85.6 %copy-start.38 = (f32[1024]{0:T(1024)S(1)}, f32[1024]{0:T(1024)}, u32[]{:S(2)}) copy-start(f32[1024]{0:T(1024)} %copy-done.37) | copy-start | bytes 12292
  468.2 85.6 %copy-start.44 = (f32[1024]{0:T(1024)S(1)}, f32[1024]{0:T(1024)}, u32[]{:S(2)}) copy-start(f32[1024]{0:T(1024)} %param.32) | copy-start | bytes 12292
  468.2 90.4 %copy-start.50 = (f32[1024]{0:T(1024)S(1)}, f32[1024]{0:T(1024)}, u32[]{:S(2)}) copy-start(f32[1024]{0:T(1024)} %copy-done.49) | copy-start | bytes 12292
  468.2 142.6 %copy-start.57 = (f32[1024]{0:T(1024)S(1)}, f32[1024]{0:T(1024)}, u32[]{:S(2)}) copy-start(f32[1024]{0:T(1024)} %param.37) | copy-start | bytes 12292
  468.3 142.6 %copy-start.61 = (f32[1024]{0:T(1024)S(1)}, f32[1024]{0:T(1024)}, u32[]{:S(2)}) copy-start(f32[1024]{0:T(1024)} %param.38) | copy-start | bytes 12292
  468.3 208.7 %all-gather.11.cloned.1.call-start = ((), (), s32[]{:S(2)}) async-start(), calls=%async_computation.10 | async-start | bytes 6291456 | tf_op jit(solution)/shard_map/all_gather | solution.py:155
  558.7 58.2 %copy-start.17 = (bf16[1024,1024]{1,0:T(8,128)(2,1)S(1)}, bf16[1024,1024]{1,0:T(8,128)(2,1)}, u32[]{:S(2)}) copy-start(bf16[1024,1024]{1,0:T(8,128)(2,1)} %param.39) | copy-start | bytes 6291460
  558.7 58.2 %copy-start.54 = (f32[1024]{0:T(1024)S(1)}, f32[1024]{0:T(1024)}, u32[]{:S(2)}) copy-start(f32[1024]{0:T(1024)} %param.31) | copy-start | bytes 12292
  620.1 551.3 %all-reduce.5.cloned.1.call-start = ((), (), s32[]{:S(2)}) async-start(), calls=%async_computation.12 | async-start | bytes 25165824 | tf_op jit(solution)/shard_map/psum | solution.py:215
  620.2 14.4 %copy-start.68 = (bf16[2048,1024]{1,0:T(8,128)(2,1)S(1)}, bf16[2048,1024]{1,0:T(8,128)(2,1)}, u32[]{:S(2)}) copy-start(bf16[2048,1024]{1,0:T(8,128)(2,1)} %all-gather.7.cloned.1.call-done) | copy-start | bytes 12582916
  732.3 7.0 copy-start.2
  732.3 7.0 copy-start.3
  772.7 7.0 copy-start.2
  772.7 7.0 copy-start.3
  833.4 7.0 copy-start.2
  833.4 7.0 copy-start.3
  873.7 7.0 copy-start.2
  873.7 7.0 copy-start.3
  936.4 292.2 %reduce-scatter.11.cloned.1.call-start = ((), (), s32[]{:S(2)}) async-start(), calls=%async_computation.11 | async-start | bytes 6291456 | tf_op jit(solution)/shard_map/reduce_scatter | solution.py:203
  1179.5 7.5 copy-start.25
  1187.0 41.6 %copy-start.9 = (bf16[1024,1024]{1,0:T(8,128)(2,1)S(1)}, bf16[1024,1024]{1,0:T(8,128)(2,1)}, u32[]{:S(2)}) copy-start(bf16[1024,1024]{1,0:T(8,128)(2,1)} %param.24) | copy-start | bytes 6291460
  1187.0 41.6 %copy-start.34 = (f32[1024]{0:T(1024)S(1)}, f32[1024]{0:T(1024)}, u32[]{:S(2)}) copy-start(f32[1024]{0:T(1024)} %copy-done.33) | copy-start | bytes 12292
  1187.0 41.6 %copy-start.42 = (f32[1024]{0:T(1024)S(1)}, f32[1024]{0:T(1024)}, u32[]{:S(2)}) copy-start(f32[1024]{0:T(1024)} %param.25) | copy-start | bytes 12292
  1191.5 40.2 %copy-start.48 = (f32[1024]{0:T(1024)S(1)}, f32[1024]{0:T(1024)}, u32[]{:S(2)}) copy-start(f32[1024]{0:T(1024)} %copy-done.47) | copy-start | bytes 12292
  1191.5 40.3 %copy-start.40 = (f32[1024]{0:T(1024)S(1)}, f32[1024]{0:T(1024)}, u32[]{:S(2)}) copy-start(f32[1024]{0:T(1024)} %copy-done.39) | copy-start | bytes 12292
  1191.5 44.4 %copy-start.46 = (f32[1024]{0:T(1024)S(1)}, f32[1024]{0:T(1024)}, u32[]{:S(2)}) copy-start(f32[1024]{0:T(1024)} %copy-done.45) | copy-start | bytes 12292
  1191.5 44.4 %copy-start.56 = (f32[1024]{0:T(1024)S(1)}, f32[1024]{0:T(1024)}, u32[]{:S(2)}) copy-start(f32[1024]{0:T(1024)} %param.30) | copy-start | bytes 12292
  1191.5 44.4 %copy-start.58 = (f32[1024]{0:T(1024)S(1)}, f32[1024]{0:T(1024)}, u32[]{:S(2)}) copy-start(f32[1024]{0:T(1024)} %param.37) | copy-start | bytes 12292
  1228.6 7.3 copy-start.11
  1228.6 7.3 copy-start.18
  1228.6 7.3 copy-start.19
  1235.9 6.8 copy-start.51
  1236.0 46.5 %copy-start.1 = (bf16[512,1024]{1,0:T(8,128)(2,1)S(1)}, bf16[512,1024]{1,0:T(8,128)(2,1)}, u32[]{:S(2)}) copy-start(bf16[512,1024]{1,0:T(8,128)(2,1)} %param.29) | copy-start | bytes 3145732
  (57 other events, 185.0 us)
Sparse Core Ops, SparseCore 0:
  15.2 58.8 all-gather.4
  194.6 99.2 reduce-scatter.4
  301.7 56.7 all-gather.6
  360.5 56.7 all-gather.8
  454.5 99.2 reduce-scatter.8
  556.5 54.2 reduce-scatter.6
  620.2 56.7 all-gather.10
  936.5 234.7 all-reduce.4
  1173.8 54.7 reduce-scatter.10
where the time goes:
time: 1300 us; the launch traced here: 1290 us
  waiting for transfers between devices  603 us (46%)
  matrix products  318 us (24%)
  local copies, waits for them, and re-layouts  154 us (12%)
  other arithmetic  126 us (10%)
  blocking collectives  72.1 us (6%)
  between operations  14.8 us (1%)
    psum x1, waiting for transfers between devices, body(): lax.psum(grad_qkv_weight.astype(jnp.bfloat16), 'dp').astype(jnp.float32)  182 us
    reduce_scatter x1, waiting for transfers between devices, body(): lax.psum_scatter(jnp.dot(mixed, out_weight, preferred_element_type=jnp.fl...  99.3 us
    reduce_scatter x1, waiting for transfers between devices, body(): lax.psum_scatter(jnp.dot(grad_pre, up_weight.T, preferred_element_type=jn...  85.4 us
    all_gather x1, waiting for transfers between devices, body(): normed = lax.all_gather(first_norm, 'tensor', axis=0, tiled=True)  54.2 us
    all_gather x1, waiting for transfers between devices, body(): normed_second = lax.all_gather(second_norm, 'tensor', axis=0, tiled=True)  54.1 us
    reduce_scatter x1, waiting for transfers between devices, body(): lax.psum_scatter(jnp.dot(hidden, down_weight, preferred_element_type=jnp....  52.1 us
    dot_general x1, matrix products, body(): jnp.dot(normed_second, up_weight, preferred_element_type=jnp.float32)  49.6 us
    convert_element_type x4, other arithmetic, attend_backward(): grad_scores = (probs * (grad_probs - delta)).astype(jnp.bfloat16)  41.6 us
  transfers between devices with their start and end apart: 9, of which 9 were waited for; matrix products, arithmetic and copies ran while one was open for 11% of the time, Pallas kernels for 0%

commit v1 on v0

--- a/solution.py
+++ b/solution.py
@@ -1,6 +1,10 @@
+import math
+
 import jax
 import jax.numpy as jnp
 from jax import lax
+from jax.experimental import pallas as pl
+from jax.experimental.pallas import tpu as pltpu
 from jax.sharding import PartitionSpec as P
 
 HD = 64
@@ -56,7 +60,7 @@
     return ((grad_keys, grad_values), grad_query)
 
 
-def body(
+def general_body(
     tokens,
     first_gain,
     first_bias,
@@ -252,6 +256,358 @@
     )
 
 
+CHUNK = 256
+PAIR = 2 * HD
+
+
+def contract(left, right):
+    return jnp.dot(left, right, preferred_element_type=jnp.float32)
+
+
+def contract_last(left, right):
+    return lax.dot_general(left, right, (((1,), (1,)), ((), ())), preferred_element_type=jnp.float32)
+
+
+def contract_first(left, right):
+    return lax.dot_general(left, right, (((0,), (0,)), ((), ())), preferred_element_type=jnp.float32)
+
+
+def turned(values):
+    return values.astype(jnp.float32).T.astype(jnp.bfloat16)
+
+
+def pair_forward(query_ref, keys_ref, values_ref, mixed_ref, logs_ref):
+    keys = keys_ref[...]
+    query_t = turned(query_ref[...] * jnp.bfloat16(HD**-0.5))
+    values_t = turned(values_ref[...])
+    row_head = lax.broadcasted_iota(jnp.int32, (PAIR, SEQ), 0) // HD
+    for head in range(2):
+        own_query = jnp.where(row_head == head, query_t, jnp.zeros_like(query_t))
+        own_values = values_t[head * HD : (head + 1) * HD]
+        parts = []
+        for start in range(0, SEQ, CHUNK):
+            scores = contract(keys, own_query[:, start : start + CHUNK])
+            peak = jnp.max(scores, axis=0, keepdims=True)
+            powers = jnp.exp(scores - peak)
+            totals = jnp.sum(powers, axis=0, keepdims=True)
+            parts.append(contract(own_values, powers.astype(jnp.bfloat16)) / totals)
+            logs_ref[0, head : head + 1, start : start + CHUNK] = peak + jnp.log(totals)
+        mixed_ref[:, head * HD : (head + 1) * HD] = jnp.concatenate(parts, axis=1).T.astype(jnp.bfloat16)
+
+
+def pair_backward(
+    query_ref, keys_ref, values_ref, grad_ref, logs_ref, dq_ref, dk_ref, dv_ref, dk_sum, dv_sum
+):
+    keys = keys_ref[...]
+    values = values_ref[...]
+    grad = grad_ref[...]
+    query = query_ref[...] * jnp.bfloat16(HD**-0.5)
+    query_t = turned(query)
+    grad_t = turned(grad)
+    keys_t = turned(keys)
+    row_head = lax.broadcasted_iota(jnp.int32, (PAIR, SEQ), 0) // HD
+    lane_head = lax.broadcasted_iota(jnp.int32, (SEQ, PAIR), 1) // HD
+    zero = jnp.zeros_like(query)
+    zero_t = jnp.zeros_like(query_t)
+    for head in range(2):
+        own_query_t = jnp.where(row_head == head, query_t, zero_t)
+        own_grad_t = jnp.where(row_head == head, grad_t, zero_t)
+        own_query = jnp.where(lane_head == head, query, zero)
+        own_grad = jnp.where(lane_head == head, grad, zero)
+        own_keys_t = keys_t[head * HD : (head + 1) * HD]
+        parts = []
+        for start in range(0, SEQ, CHUNK):
+            cut = slice(start, start + CHUNK)
+            scores = contract(keys, own_query_t[:, cut])
+            probs = jnp.exp(scores - logs_ref[0, head : head + 1, cut])
+            grad_probs = contract(values, own_grad_t[:, cut])
+            delta = jnp.sum(grad_probs * probs, axis=0, keepdims=True)
+            grad_scores = (probs * (grad_probs - delta)).astype(jnp.bfloat16)
+            dv_part = contract(probs.astype(jnp.bfloat16), own_grad[cut])
+            dk_part = contract(grad_scores, own_query[cut])
+            if head == 0 and start == 0:
+                dv_sum[...] = dv_part
+                dk_sum[...] = dk_part
+            else:
+                dv_sum[...] += dv_part
+                dk_sum[...] += dk_part
+            parts.append(contract(own_keys_t, grad_scores) * HD**-0.5)
+        dq_ref[:, head * HD : (head + 1) * HD] = jnp.concatenate(parts, axis=1).T.astype(jnp.bfloat16)
+    dk_ref[...] = dk_sum[...].astype(jnp.bfloat16)
+    dv_ref[...] = dv_sum[...].astype(jnp.bfloat16)
+
+
+def part_spec(offset):
+    return pl.BlockSpec((SEQ, PAIR), lambda image, pair: (image, offset + pair))
+
+
+def logs_spec(pairs):
+    return pl.BlockSpec((1, 2, SEQ), lambda image, pair: (image * pairs + pair, 0, 0))
+
+
+def attend(projected):
+    rows, columns = projected.shape[0], projected.shape[1] // 3
+    pairs, images = columns // PAIR, rows // SEQ
+    area = images * columns // HD * SEQ * SEQ
+    return pl.pallas_call(
+        pair_forward,
+        grid=(images, pairs),
+        in_specs=[part_spec(0), part_spec(pairs), part_spec(2 * pairs)],
+        out_specs=[part_spec(0), logs_spec(pairs)],
+        out_shape=[
+            jax.ShapeDtypeStruct((rows, columns), jnp.bfloat16),
+            jax.ShapeDtypeStruct((images * pairs, 2, SEQ), jnp.float32),
+        ],
+        compiler_params=pltpu.CompilerParams(vmem_limit_bytes=48 * 2**20),
+        cost_estimate=pl.CostEstimate(
+            flops=16 * area * HD, bytes_accessed=8 * rows * columns, transcendentals=area
+        ),
+    )(projected, projected, projected)
+
+
+def attend_grad(projected, grad_mixed, logs):
+    rows, columns = grad_mixed.shape
+    pairs, images = columns // PAIR, rows // SEQ
+    area = images * columns // HD * SEQ * SEQ
+    return pl.pallas_call(
+        pair_backward,
+        grid=(images, pairs),
+        in_specs=[
+            part_spec(0),
+            part_spec(pairs),
+            part_spec(2 * pairs),
+            part_spec(0),
+            logs_spec(pairs),
+        ],
+        out_specs=[part_spec(0)] * 3,
+        out_shape=[jax.ShapeDtypeStruct((rows, columns), jnp.bfloat16)] * 3,
+        scratch_shapes=[pltpu.VMEM((SEQ, PAIR), jnp.float32)] * 2,
+        compiler_params=pltpu.CompilerParams(vmem_limit_bytes=48 * 2**20),
+        cost_estimate=pl.CostEstimate(
+            flops=40 * area * HD, bytes_accessed=14 * rows * columns, transcendentals=area
+        ),
+    )(projected, projected, projected, grad_mixed, logs)
+
+
+def over_group(values):
+    return lax.ppermute(values, "tensor", [(0, 1), (1, 0)])
+
+
+def over_pair(values):
+    size = lax.axis_size("dp")
+    return lax.ppermute(values, "dp", [(index, index ^ 1) for index in range(size)])
+
+
+def fetch(weight, axis, parity):
+    half = weight.shape[axis] // 2
+    near = over_group(lax.dynamic_slice_in_dim(weight, parity * half, half, axis))
+    return jnp.concatenate([near, over_pair(near)], axis=axis)
+
+
+def sum_everywhere(own, other, axis, parity, after):
+    half = own.shape[axis] // 2
+    keep = lax.dynamic_slice_in_dim(own, parity * half, half, axis)
+    give = lax.dynamic_slice_in_dim(own, (1 - parity) * half, half, axis)
+    other_keep = lax.slice_in_dim(other, 0, half, axis=axis)
+    other_give = lax.slice_in_dim(other, half, 2 * half, axis=axis)
+    other_sum = other_keep + over_pair(other_give)
+    own_sum = keep + over_pair(give)
+    quarter = own_sum + over_group(other_sum)
+    if after is not None:
+        quarter, after = lax.optimization_barrier((quarter, after))
+    size = lax.axis_size("dp")
+    groups = [list(range(0, size, 2)), list(range(1, size, 2))]
+    return lax.psum(quarter, "dp", axis_index_groups=groups), after
+
+
+def both_halves(summed, axis, parity):
+    partner = over_pair(summed)
+    low = jnp.where(parity == 0, summed, partner)
+    high = jnp.where(parity == 0, partner, summed)
+    return jnp.concatenate([low, high], axis=axis).astype(jnp.float32)
+
+
+def image_body(
+    tokens,
+    first_gain,
+    first_bias,
+    qkv_weight,
+    qv_bias,
+    out_weight,
+    out_bias,
+    attention_scale,
+    second_gain,
+    second_bias,
+    up_weight,
+    up_bias,
+    down_weight,
+    down_bias,
+    mlp_scale,
+    cotangent,
+):
+    width = tokens.shape[1]
+    columns = qkv_weight.shape[2]
+    units = up_weight.shape[1]
+    parity = lax.axis_index("dp") % 2
+    low = jnp.bfloat16
+
+    def in_order(values):
+        half = values.shape[-1] // 2
+        turned_round = jnp.concatenate([values[..., half:], values[..., :half]], axis=-1)
+        return jnp.where(parity == 0, values, turned_round)
+
+    qkv_own = qkv_weight.reshape(width, 3 * columns)
+    half = columns // 2
+    sent = jnp.concatenate(
+        [
+            lax.dynamic_slice_in_dim(qkv_own, j * columns + parity * half, half, 1)
+            for j in range(3)
+        ],
+        axis=1,
+    )
+    near = over_group(sent)
+    far = over_pair(near)
+    qkv_other = jnp.concatenate(
+        [piece[:, j * half : (j + 1) * half] for j in range(3) for piece in (near, far)], axis=1
+    )
+    biases = over_group(jnp.concatenate([qv_bias.reshape(-1), up_bias]))
+    qv_other = in_order(biases[: 2 * columns].reshape(2, columns))
+    up_bias_other = in_order(biases[2 * columns :])
+    out_other = fetch(out_weight, 0, parity)
+    up_other = fetch(up_weight, 1, parity)
+    down_other = fetch(down_weight, 0, parity)
+    qkv_pair = (qkv_own, qkv_other)
+    qv_pair = (qv_bias, qv_other)
+    out_pair = (out_weight, out_other)
+    up_pair = (up_weight, up_other)
+    up_bias_pair = (up_bias, up_bias_other)
+    down_pair = (down_weight, down_other)
+
+    residual = tokens.astype(jnp.float32)
+    first_norm = norm_rows(residual, first_gain, first_bias).astype(low)
+    projected = []
+    mixed = []
+    logs = []
+    for weight, bias in zip(qkv_pair, qv_pair):
+        shift = jnp.concatenate([bias[0], jnp.zeros_like(bias[0]), bias[1]])
+        projected.append((contract(first_norm, weight) + shift).astype(low))
+        part, log_part = attend(projected[-1])
+        mixed.append(part)
+        logs.append(log_part)
+    attention = contract(mixed[0], out_pair[0]) + contract(mixed[1], out_pair[1]) + out_bias
+    after_attention = residual + attention_scale * attention
+    second_norm = norm_rows(after_attention, second_gain, second_bias).astype(low)
+    hidden = []
+    slopes = []
+    for weight, bias in zip(up_pair, up_bias_pair):
+        pre_act = contract(second_norm, weight) + bias
+        spread = 0.5 * (1.0 + lax.erf(pre_act * math.sqrt(0.5)))
+        slope = spread + pre_act * jnp.exp(-0.5 * pre_act * pre_act) * (1.0 / math.sqrt(2.0 * math.pi))
+        act, slope = lax.optimization_barrier(((pre_act * spread).astype(low), slope.astype(low)))
+        hidden.append(act)
+        slopes.append(slope)
+    feed = contract(hidden[0], down_pair[0]) + contract(hidden[1], down_pair[1]) + down_bias
+    block_out = (after_attention + mlp_scale * feed).astype(low)
+
+    upstream = cotangent.astype(jnp.float32)
+    grad_mlp_scale = jnp.sum(upstream * feed, axis=0)
+    grad_feed = (upstream * mlp_scale).astype(low)
+    grad_down_bias = jnp.sum(grad_feed.astype(jnp.float32), axis=0)
+    down_sum, _ = sum_everywhere(
+        *[contract_first(act, grad_feed).astype(low) for act in hidden], 0, parity, None
+    )
+    grad_pre = [
+        (contract_last(grad_feed, weight) * slope.astype(jnp.float32)).astype(low)
+        for weight, slope in zip(down_pair, slopes)
+    ]
+    grad_up_bias = [jnp.sum(part.astype(jnp.float32), axis=0) for part in grad_pre]
+    up_sum, down_sum = sum_everywhere(
+        *[contract_first(second_norm, part).astype(low) for part in grad_pre], 1, parity, down_sum
+    )
+    grad_second = contract_last(grad_pre[0], up_pair[0]) + contract_last(grad_pre[1], up_pair[1])
+    _, second_pull = jax.vjp(norm_rows, after_attention, second_gain, second_bias)
+    grad_after, grad_second_gain, grad_second_bias = second_pull(grad_second)
+    grad_after = grad_after + upstream
+    grad_attention_scale = jnp.sum(grad_after * attention, axis=0)
+    grad_attention = (grad_after * attention_scale).astype(low)
+    grad_out_bias = jnp.sum(grad_attention.astype(jnp.float32), axis=0)
+    out_sum, up_sum = sum_everywhere(
+        *[contract_first(part, grad_attention).astype(low) for part in mixed], 0, parity, up_sum
+    )
+    grad_projected = []
+    grad_qv = []
+    qkv_grads = []
+    for part, log_part, weight in zip(projected, logs, out_pair):
+        grad_mixed = contract_last(grad_attention, weight).astype(low)
+        parts = attend_grad(part, grad_mixed, log_part)
+        grad_qv.append(
+            jnp.stack([jnp.sum(parts[j].astype(jnp.float32), axis=0) for j in (0, 2)])
+        )
+        grad_projected.append(jnp.concatenate(parts, axis=1))
+        qkv_grads.append(jnp.stack([contract_first(first_norm, each).astype(low) for each in parts]))
+    qkv_sum, out_sum = sum_everywhere(*qkv_grads, 2, parity, out_sum)
+    grad_first = contract_last(grad_projected[0], qkv_pair[0]) + contract_last(
+        grad_projected[1], qkv_pair[1]
+    )
+    _, first_pull = jax.vjp(norm_rows, residual, first_gain, first_bias)
+    grad_input, grad_first_gain, grad_first_bias = first_pull(grad_first)
+    grad_input = grad_input + grad_after
+
+    place = lax.axis_index("tensor")
+
+    def whole(own, other):
+        other = in_order(other)
+        first = jnp.where(place == 0, own, other)
+        second = jnp.where(place == 0, other, own)
+        return jnp.concatenate([first, second], axis=-1)
+
+    shared = lax.psum(
+        jnp.concatenate(
+            [
+                grad_first_gain,
+                grad_first_bias,
+                grad_out_bias,
+                grad_attention_scale,
+                grad_second_gain,
+                grad_second_bias,
+                grad_down_bias,
+                grad_mlp_scale,
+                whole(*grad_qv).reshape(-1),
+                whole(*grad_up_bias),
+            ]
+        ),
+        ("dp", "tensor"),
+    )
+    vectors = [shared[j * width : (j + 1) * width] for j in range(8)]
+    qv_total = shared[8 * width : 8 * width + 4 * columns].reshape(2, 2 * columns)
+    up_total = shared[8 * width + 4 * columns :]
+    return (
+        block_out,
+        grad_input,
+        vectors[0],
+        vectors[1],
+        both_halves(qkv_sum, 2, parity).transpose(1, 0, 2),
+        lax.dynamic_slice_in_dim(qv_total, place * columns, columns, 1),
+        both_halves(out_sum, 0, parity),
+        vectors[2],
+        vectors[3],
+        vectors[4],
+        vectors[5],
+        both_halves(up_sum, 1, parity),
+        lax.dynamic_slice_in_dim(up_total, place * units, units, 0),
+        both_halves(down_sum, 0, parity),
+        vectors[6],
+        vectors[7],
+    )
+
+
+def body(tokens, *others):
+    fits = tokens.shape[0] % SEQ == 0 and others[2].shape[2] % (2 * PAIR) == 0
+    if fits and lax.axis_size("tensor") == 2 and lax.axis_size("dp") % 2 == 0:
+        return image_body(tokens, *others)
+    return general_body(tokens, *others)
+
+
 def solution(mesh):
     return jax.shard_map(
         body,

time: 1300 us -> 874 us (0.67)
  waiting for transfers between devices: 603 us -> 388 us
  matrix products: 318 us -> 148 us
  Pallas kernels: 0 us -> 112 us
  local copies, waits for them, and re-layouts: 154 us -> 76.8 us
  other arithmetic: 126 us -> 63.1 us
  blocking collectives: 72.1 us -> 41.6 us
  starting transfers between devices: 0.37 us -> 22.9 us
    reduce_scatter x4 -> x0, waiting for transfers between devices: 274 us -> none  [the longest x1 99.3 us: body(): lax.psum_scatter(jnp.dot(mixed, out_weight, preferred_element_type=jnp.fl...]
    ppermute x0 -> x25, waiting for transfers between devices: none -> 171 us  [the longest x9 171 us: over_group(): return lax.ppermute(values, 'tensor', [(0, 1), (1, 0)])]
    dot_general x40 -> x28, matrix products: 318 us -> 148 us  [the longest x8 61.4 us: contract(): return jnp.dot(left, right, preferred_element_type=jnp.float32)]
    all_gather x4 -> x0, waiting for transfers between devices: 147 us -> none  [the longest x1 54.2 us: body(): normed = lax.all_gather(first_norm, 'tensor', axis=0, tiled=True)]
    pallas_call x0 -> x4, Pallas kernels: none -> 112 us  [the longest x2 61.7 us: attend_grad(): pl.pallas_call(pair_backward, grid=(images, pairs), in_specs=[part_spec(0...]
    while x96 -> x0, local copies, waits for them, and re-layouts: 58.9 us -> none
    convert_element_type x12 -> x5, other arithmetic: 64.9 us -> 14.9 us  [the longest x3 12.1 us: both_halves(): return jnp.concatenate([low, high], axis=axis).astype(jnp.float32)]
    reshape x13 -> x0, local copies, waits for them, and re-layouts: 34.9 us -> none  [the longest x2 7.84 us: body(): grad_query = grad_query.reshape(total_rows, columns)]
  transfers between devices with their start and end apart: 9 -> 29, of which waited for: 9 -> 10; matrix products, arithmetic and copies ran while one was open for 11% -> 30% of each run, Pallas kernels for 0% -> 13%
where the time goes in v1:
time: 874 us; the launch traced here: 867 us
  waiting for transfers between devices  388 us (44%)
  matrix products  148 us (17%)
  Pallas kernels  112 us (13%)
  local copies, waits for them, and re-layouts  76.8 us (9%)
  other arithmetic  63.1 us (7%)
  blocking collectives  41.6 us (5%)
  starting transfers between devices  22.9 us (3%)
  between operations  15 us (2%)
    psum x4, waiting for transfers between devices, sum_everywhere(): return (lax.psum(quarter, 'dp', axis_index_groups=groups), after)  216 us
    ppermute x9, waiting for transfers between devices, over_group(): return lax.ppermute(values, 'tensor', [(0, 1), (1, 0)])  171 us
    pallas_call x2, Pallas kernels, attend_grad(): pl.pallas_call(pair_backward, grid=(images, pairs), in_specs=[part_spec(0...  61.7 us
    dot_general x8, matrix products, contract(): return jnp.dot(left, right, preferred_element_type=jnp.float32)  61.4 us
    unnamed x160, local copies, waits for them, and re-layouts  51.4 us
    dot_general x8, matrix products, contract_last(): lax.dot_general(left, right, (((1,), (1,)), ((), ())), preferred_element_...  51.3 us
    pallas_call x2, Pallas kernels, attend(): pl.pallas_call(pair_forward, grid=(images, pairs), in_specs=[part_spec(0)...  50.2 us
    psum x1, blocking collectives, image_body(): lax.psum(jnp.concatenate([grad_first_gain, grad_first_bias, grad_out_bias...  41.6 us
  transfers between devices with their start and end apart: 29, of which 10 were waited for; matrix products, arithmetic and copies ran while one was open for 30% of the time, Pallas kernels for 13%

profile of v1, /device:TPU:1, one launch (start us, length us, event | category | flops | bytes accessed | tf_op | source)
XLA Modules:
  0.0 867.1 jit_solution(12212025234835765457)
XLA Ops:
  10.8 4.6 copy.43
  33.3 3.9 copy.46
  37.3 6.0 add_convert_fusion.1.query_ref.keys_ref.values_ref
  43.3 10.1 %collective-permute-done = bf16[1024,768]{0,1:T(8,128)(2,1)} collective-permute-done((bf16[1024,768]{0,1:T(8,128)(2,1)}, bf16[1024,768]{0,1:T(8,128)(2,1)}, u32[]{:S(2)}, u32[]{:S(2)}) %collective-permute-start) | collective-permute-done | bytes 1572896 | tf_op jit(solution)/shard_map/ppermute | solution.py:393
  53.4 3.4 collective-permute-start.1
  56.8 25.0 %shard_map.279 = (bf16[1024,512]{1,0:T(8,128)(2,1)S(1)}, f32[4,2,1024]{2,1,0:T(2,128)S(1)}) custom-call(bf16[1024,1536]{1,0:T(8,128)(2,1)S(1)} %add_convert_fusion.1.query_ref.keys_ref.values_ref, bf16[1024,1536]{1,0:T(8,128)(2,1)S(1)} %add_convert_fusion.1.query_ref.keys_ref.values_ref, bf16[1024,1536]{1,0:T(8,128)(2,1)S(1)} %add_convert_fusion.1.query_ref.keys_ref.values_ref), custom_call_target="tpu_custom_call" | custom-call | flops 8589934592 | bytes 4194304 | tf_op jit(solution)/shard_map/pallas_call | solution.py:352
  85.4 24.2 %collective-permute-done.5 = bf16[1024,1024]{1,0:T(8,128)(2,1)} collective-permute-done((bf16[1024,1024]{1,0:T(8,128)(2,1)}, bf16[1024,1024]{1,0:T(8,128)(2,1)}, u32[]{:S(2)}, u32[]{:S(2)}) %collective-permute-start.5) | collective-permute-done | bytes 2097184 | tf_op jit(solution)/shard_map/ppermute | solution.py:393
  109.5 3.4 collective-permute-start.6
  112.9 41.5 %collective-permute-done.7 = bf16[1024,1024]{1,0:T(8,128)(2,1)} collective-permute-done((bf16[1024,1024]{1,0:T(8,128)(2,1)}, bf16[1024,1024]{1,0:T(8,128)(2,1)}, u32[]{:S(2)}, u32[]{:S(2)}) %collective-permute-start.7) | collective-permute-done | bytes 2097184 | tf_op jit(solution)/shard_map/ppermute | solution.py:393
  159.5 3.3 constant_dynamic-update-slice_fusion.5
  169.8 3.8 add_convert_fusion.query_ref.keys_ref.values_ref
  173.6 25.2 %shard_map.280 = (bf16[1024,512]{1,0:T(8,128)(2,1)S(1)}, f32[4,2,1024]{2,1,0:T(2,128)S(1)}) custom-call(bf16[1024,1536]{1,0:T(8,128)(2,1)S(1)} %add_convert_fusion.query_ref.keys_ref.values_ref, bf16[1024,1536]{1,0:T(8,128)(2,1)S(1)} %add_convert_fusion.query_ref.keys_ref.values_ref, bf16[1024,1536]{1,0:T(8,128)(2,1)S(1)} %add_convert_fusion.query_ref.keys_ref.values_ref), custom_call_target="tpu_custom_call" | custom-call | flops 8589934592 | bytes 4194304 | tf_op jit(solution)/shard_map/pallas_call | solution.py:352
  198.9 3.3 fusion.60
  205.8 9.3 %fusion.4 = (bf16[1024,2048]{1,0:T(8,128)(2,1)}, bf16[1024,2048]{1,0:T(8,128)(2,1)}) fusion(f32[2048]{0:T(1024)S(1)} %copy-done.57, bf16[1024,1024]{0,1:T(8,128)(2,1)S(1)} %add_convert_fusion.3, bf16[1024,2048]{1,0:T(8,128)(2,1)S(1)} %copy-done.34), kind=kOutput, calls=%fused_computation.6 | convolution fusion | flops 4320133120 | bytes 14688256 | tf_op jit(solution)/shard_map/dot_general | solution.py:264
  215.1 10.1 %convert_reduce_fusion.1 = (f32[2048]{0:T(1024)}, bf16[1024,2048]{1,0:T(8,128)(2,1)}) fusion(bf16[1024,2048]{1,0:T(8,128)(2,1)} %get-tuple-element.40, bf16[2048,1024]{1,0:T(8,128)(2,1)} %param.28, bf16[1024,1024]{0,1:T(8,128)(2,1)S(1)} %copy-done.12, f32[1024]{0:T(1024)S(1)} %copy-done.63), kind=kOutput, calls=%fused_computation.13 | convolution fusion | flops 4308596736 | bytes 14692352 | tf_op jit(solution)/shard_map/dot_general | solution.py:268
  225.2 7.1 convolution_convert_fusion.3
  237.2 5.6 convolution_convert_fusion.1
  247.7 6.1 fusion.69
  253.8 8.4 fusion.68
  265.3 11.8 %fusion.9 = (bf16[1024,2048]{1,0:T(8,128)(2,1)}, bf16[1024,2048]{1,0:T(8,128)(2,1)}) fusion(f32[2048]{0:T(1024)S(1)} %slice_select_fusion, bf16[1024,1024]{0,1:T(8,128)(2,1)S(1)} %add_convert_fusion.3, bf16[1024,2048]{1,0:T(8,128)(2,1)} %constant_dynamic-update-slice_fusion.2), kind=kOutput, calls=%fused_computation.11 | convolution fusion | flops 4320133120 | bytes 14688256 | tf_op jit(solution)/shard_map/dot_general | solution.py:264
  278.8 10.7 %convert_reduce_fusion = (f32[2048]{0:T(1024)}, bf16[1024,2048]{1,0:T(8,128)(2,1)}) fusion(bf16[1024,2048]{1,0:T(8,128)(2,1)} %get-tuple-element.41, bf16[2048,1024]{1,0:T(8,128)(2,1)S(1)} %constant_dynamic-update-slice_fusion.4, bf16[1024,1024]{0,1:T(8,128)(2,1)S(1)} %copy-done.12, f32[1024]{0:T(1024)S(1)} %copy-done.63), kind=kOutput, calls=%fused_computation.12 | convolution fusion | flops 4308596736 | bytes 14692352 | tf_op jit(solution)/shard_map/dot_general | solution.py:268
  289.6 10.8 %multiply_reduce_fusion = (f32[1024]{0:T(1024)}, f32[1024]{0:T(1024)S(1)}, f32[1024]{0:T(1024)}, f32[1024,1024]{0,1:T(8,128)S(1)}) fusion(f32[1024,1024]{0,1:T(8,128)S(1)} %get-tuple-element.103, f32[1024]{0:T(1024)S(1)} %fusion.49, f32[1024]{0:T(1024)S(1)} %broadcast_multiply_fusion, f32[1024]{0:T(1024)S(1)} %copy-done.51, f32[1024,1024]{0,1:T(8,128)} %fusion.69, ...), kind=kOutput, calls=%fused_computation.47 | convolution fusion | flops 4304401408 | bytes 20996096 | tf_op jit(solution)/shard_map/dot_general | solution.py:268
  308.3 4.9 convolution_convert_fusion.2
  313.2 31.0 %shard_map.282 = (bf16[1024,512]{1,0:T(8,128)(2,1)S(1)}, bf16[1024,512]{1,0:T(8,128)(2,1)S(1)}, bf16[1024,512]{1,0:T(8,128)(2,1)S(1)}) custom-call(bf16[1024,1536]{1,0:T(8,128)(2,1)} %copy-done.5, bf16[1024,1536]{1,0:T(8,128)(2,1)} %copy-done.5, bf16[1024,1536]{1,0:T(8,128)(2,1)} %copy-done.5, bf16[1024,512]{1,0:T(8,128)(2,1)S(1)} %convolution_convert_fusion.12.grad_ref, ...), custom_call_target="tpu_custom_call" | custom-call | flops 21474836480 | bytes 7340032 | tf_op jit(solution)/shard_map/pallas_call | solution.py:372
  353.2 5.8 convolution_convert_fusion
  361.7 30.7 %shard_map.281 = (bf16[1024,512]{1,0:T(8,128)(2,1)S(1)}, bf16[1024,512]{1,0:T(8,128)(2,1)S(1)}, bf16[1024,512]{1,0:T(8,128)(2,1)S(1)}) custom-call(bf16[1024,1536]{1,0:T(8,128)(2,1)} %copy-done.4, bf16[1024,1536]{1,0:T(8,128)(2,1)} %copy-done.4, bf16[1024,1536]{1,0:T(8,128)(2,1)} %copy-done.4, bf16[1024,512]{1,0:T(8,128)(2,1)S(1)} %convolution_convert_fusion.13.grad_ref, ...), custom_call_target="tpu_custom_call" | custom-call | flops 21474836480 | bytes 7340032 | tf_op jit(solution)/shard_map/pallas_call | solution.py:372
  399.5 5.0 fusion.23
  404.5 3.4 slice_add_fusion
  408.1 6.0 fusion.58
  419.6 35.9 %collective-permute-done.20 = bf16[1024,1024]{1,0:T(8,128)(2,1)} collective-permute-done((bf16[1024,1024]{1,0:T(8,128)(2,1)}, bf16[1024,1024]{1,0:T(8,128)(2,1)}, u32[]{:S(2)}, u32[]{:S(2)}) %collective-permute-start.20) | collective-permute-done | bytes 2097184 | tf_op jit(solution)/shard_map/ppermute | solution.py:393
  455.5 5.0 add_add_fusion.5
  460.6 17.7 %fusion.22 = (f32[1024]{0:T(1024)S(1)}, f32[1024]{0:T(1024)S(1)}, f32[1024]{0:T(1024)S(1)}, f32[1024,1024]{0,1:T(8,128)}, bf16[1024,1024]{0,1:T(8,128)(2,1)}) fusion(bf16[1024,1024]{0,1:T(8,128)(2,1)} %copy.46, f32[1024]{0:T(1024)S(1)} %copy-done.63, f32[1024,1024]{0,1:T(8,128)} %get-tuple-element.146, f32[1024,1024]{0,1:T(8,128)} %copy-done.9, ...), kind=kOutput, calls=%fused_computation.43 | convolution fusion | flops 4321178624 | bytes 39890944 | tf_op jit(solution)/shard_map/dot_general | solution.py:264
  478.3 3.4 convolution_convert_fusion.5
  484.7 17.6 %collective-permute-done.17 = bf16[1024,1024]{1,0:T(8,128)(2,1)} collective-permute-done((bf16[1024,1024]{1,0:T(8,128)(2,1)}, bf16[1024,1024]{1,0:T(8,128)(2,1)}, u32[]{:S(2)}, u32[]{:S(2)}) %collective-permute-start.17) | collective-permute-done | bytes 2097184 | tf_op jit(solution)/shard_map/ppermute | solution.py:393
  502.3 5.0 add_add_fusion.6
  507.3 56.7 %all-reduce.5.cloned.1.call-done = bf16[1024,1024]{1,0:T(8,128)(2,1)} async-done(((bf16[1024,1024]{1,0:T(8,128)(2,1)}), bf16[1024,1024]{1,0:T(8,128)(2,1)}) %all-reduce.5.cloned.1.call-update) | async-done | bytes 2097168 | tf_op jit(solution)/shard_map/psum | solution.py:420
  565.8 3.3 slice_add_fusion.2
  573.7 41.8 %collective-permute-done.14 = bf16[256,1024]{1,0:T(8,128)(2,1)S(1)} collective-permute-done((bf16[256,1024]{1,0:T(8,128)(2,1)S(1)}, bf16[256,1024]{1,0:T(8,128)(2,1)S(1)}, u32[]{:S(2)}, u32[]{:S(2)}) %collective-permute-start.14) | collective-permute-done | bytes 524320 | tf_op jit(solution)/shard_map/ppermute | solution.py:393
  617.7 52.2 %all-reduce.7.cloned.1.call-done = bf16[1024,1024]{1,0:T(8,128)(2,1)} async-done(((bf16[1024,1024]{1,0:T(8,128)(2,1)}), bf16[1024,1024]{1,0:T(8,128)(2,1)}) %all-reduce.7.cloned.1.call-update) | async-done | bytes 2097168 | tf_op jit(solution)/shard_map/psum | solution.py:420
  670.0 4.2 add_add_fusion.7
  674.2 70.2 %all-reduce.9.cloned.1.call-done = bf16[256,1024]{1,0:T(8,128)(2,1)} async-done(((bf16[256,1024]{1,0:T(8,128)(2,1)}), bf16[256,1024]{1,0:T(8,128)(2,1)}) %all-reduce.9.cloned.1.call-update) | async-done | bytes 524304 | tf_op jit(solution)/shard_map/psum | solution.py:420
  747.0 41.6 %psum.35 = f32[14336]{0:T(1024)S(1)} all-reduce(f32[14336]{0:T(1024)S(1)} %select_dynamic-update-slice_fusion), channel_id=1, replica_groups=mesh['dp'=16,'tensor'=2] {'dp','tensor'}, use_global_device_ids=true, to_apply=%region_22.23 | all-reduce | flops 14336 | bytes 114688 | tf_op jit(solution)/shard_map/psum | solution.py:564
  791.2 5.4 copy.52
  799.4 3.9 broadcast_select_fusion.1
  803.3 37.2 %all-reduce.11.cloned.1.call-done = bf16[3,1024,256]{2,1,0:T(8,128)(2,1)} async-done(((bf16[3,1024,256]{2,1,0:T(8,128)(2,1)}), bf16[3,1024,256]{2,1,0:T(8,128)(2,1)}) %all-reduce.11.cloned.1.call-update) | async-done | bytes 1572880 | tf_op jit(solution)/shard_map/psum | solution.py:420
  841.0 6.2 maximum_convert_fusion.1
  852.1 4.4 maximum_convert_fusion
  856.8 3.6 convert_bitcast_fusion
  (282 shorter events, 112.6 us)
Async XLA Ops:
  7.2 556.9 %all-reduce.5.cloned.1.call-start = ((), (), s32[]{:S(2)}) async-start(), calls=%async_computation | async-start | bytes 4194304 | tf_op jit(solution)/shard_map/psum | solution.py:420
  8.7 28.5 %collective-permute-start.2 = (f32[3072]{0:T(1024)S(1)}, f32[3072]{0:T(1024)S(1)}, u32[]{:S(2)}, u32[]{:S(2)}) collective-permute-start(f32[3072]{0:T(1024)S(1)} %pad_maximum_fusion.3), channel_id=1, source_target_pairs={{0,1},{1,0},{2,3},{3,2},{4,5},{5,4},{6,7},{7,6},{8,9},{9,8},{10,11... | collective-permute-start | bytes 36872 | tf_op jit(solution)/shard_map/ppermute | solution.py:393
  18.1 35.2 %collective-permute-start = (bf16[1024,768]{0,1:T(8,128)(2,1)}, bf16[1024,768]{0,1:T(8,128)(2,1)}, u32[]{:S(2)}, u32[]{:S(2)}) collective-permute-start(bf16[1024,768]{0,1:T(8,128)(2,1)} %pad_maximum_fusion.2), channel_id=1, source_target_pairs={{0,1},{1,0},{2,3},{3,2},{4,5},{5,4},{6,7},{7,6},{8,9},{9,8},{10,11... | collective-permute-start | bytes 4718600 | tf_op jit(solution)/shard_map/ppermute | solution.py:393
  19.0 62.8 %collective-permute-start.3 = (bf16[256,1024]{1,0:T(8,128)(2,1)}, bf16[256,1024]{1,0:T(8,128)(2,1)}, u32[]{:S(2)}, u32[]{:S(2)}) collective-permute-start(bf16[256,1024]{1,0:T(8,128)(2,1)} %constant_dynamic-slice_fusion.7), channel_id=1, source_target_pairs={{0,1},{1,0},{2,3},{3,2},{4,5},{5,4},{6,7},{7,6},{8,9},{9,8},{10,11... | collective-permute-start | bytes 1572872 | tf_op jit(solution)/shard_map/ppermute | solution.py:393
  23.7 85.9 %collective-permute-start.5 = (bf16[1024,1024]{1,0:T(8,128)(2,1)}, bf16[1024,1024]{1,0:T(8,128)(2,1)}, u32[]{:S(2)}, u32[]{:S(2)}) collective-permute-start(bf16[1024,1024]{1,0:T(8,128)(2,1)} %constant_dynamic-slice_fusion.6), channel_id=1, source_target_pairs={{0,1},{1,0},{2,3},{3,2},{4,5},{5,4},{6,7},{7,6},{8,9},{9,8},{10,11... | collective-permute-start | bytes 6291464 | tf_op jit(solution)/shard_map/ppermute | solution.py:393
  25.2 129.3 %collective-permute-start.7 = (bf16[1024,1024]{1,0:T(8,128)(2,1)}, bf16[1024,1024]{1,0:T(8,128)(2,1)}, u32[]{:S(2)}, u32[]{:S(2)}) collective-permute-start(bf16[1024,1024]{1,0:T(8,128)(2,1)} %constant_dynamic-slice_fusion.5), channel_id=1, source_target_pairs={{0,1},{1,0},{2,3},{3,2},{4,5},{5,4},{6,7},{7,6},{8,9},{9,8},{10,11... | collective-permute-start | bytes 6291464 | tf_op jit(solution)/shard_map/ppermute | solution.py:393
  29.5 169.4 %copy-start.6 = (bf16[1024,1024]{0,1:T(8,128)(2,1)}, bf16[1024,1024]{0,1:T(8,128)(2,1)S(1)}, u32[]{:S(2)}) copy-start(bf16[1024,1024]{0,1:T(8,128)(2,1)S(1)} %copy.42) | copy-start | bytes 6291460
  43.3 38.4 %copy-start.4 = (bf16[1024,1536]{1,0:T(8,128)(2,1)}, bf16[1024,1536]{1,0:T(8,128)(2,1)S(1)}, u32[]{:S(2)}) copy-start(bf16[1024,1536]{1,0:T(8,128)(2,1)S(1)} %add_convert_fusion.1.query_ref.keys_ref.values_ref) | copy-start | bytes 9437188
  53.4 109.4 %collective-permute-start.1 = (bf16[1024,768]{0,1:T(8,128)(2,1)}, bf16[1024,768]{0,1:T(8,128)(2,1)}, u32[]{:S(2)}, u32[]{:S(2)}) collective-permute-start(bf16[1024,768]{0,1:T(8,128)(2,1)} %collective-permute-done), channel_id=1, source_target_pairs={{0,2},{2,0},{4,6},{6,4},{8,10},{10,8},{12,14},{14,12},{16,18},{18,... | collective-permute-start | bytes 4718600 | tf_op jit(solution)/shard_map/ppermute | solution.py:398
  81.7 2.5 collective-permute-start.4
  109.5 152.7 %collective-permute-start.6 = (bf16[1024,1024]{1,0:T(8,128)(2,1)}, bf16[1024,1024]{1,0:T(8,128)(2,1)}, u32[]{:S(2)}, u32[]{:S(2)}) collective-permute-start(bf16[1024,1024]{1,0:T(8,128)(2,1)} %collective-permute-done.5), channel_id=1, source_target_pairs={{0,2},{2,0},{4,6},{6,4},{8,10},{10,8},{12,14},{14,12},{16,18},{18,... | collective-permute-start | bytes 6291464 | tf_op jit(solution)/shard_map/ppermute | solution.py:398
  154.5 122.6 %collective-permute-start.8 = (bf16[1024,1024]{1,0:T(8,128)(2,1)}, bf16[1024,1024]{1,0:T(8,128)(2,1)}, u32[]{:S(2)}, u32[]{:S(2)}) collective-permute-start(bf16[1024,1024]{1,0:T(8,128)(2,1)} %collective-permute-done.7), channel_id=1, source_target_pairs={{0,2},{2,0},{4,6},{6,4},{8,10},{10,8},{12,14},{14,12},{16,18},{18,... | collective-permute-start | bytes 6291464 | tf_op jit(solution)/shard_map/ppermute | solution.py:398
  173.6 25.3 %copy-start.52 = (f32[1024]{0:T(1024)S(1)}, f32[1024]{0:T(1024)}, u32[]{:S(2)}) copy-start(f32[1024]{0:T(1024)} %param.23) | copy-start | bytes 12292
  173.6 25.3 %copy-start.58 = (f32[1024]{0:T(1024)S(1)}, f32[1024]{0:T(1024)}, u32[]{:S(2)}) copy-start(f32[1024]{0:T(1024)} %param.22) | copy-start | bytes 12292
  202.1 98.2 %copy-start.8 = (f32[1024,1024]{0,1:T(8,128)}, f32[1024,1024]{0,1:T(8,128)S(1)}, u32[]{:S(2)}) copy-start(f32[1024,1024]{0,1:T(8,128)S(1)} %get-tuple-element.103) | copy-start | bytes 12582916
  235.8 247.7 %collective-permute-start.15 = (bf16[1024,1024]{1,0:T(8,128)(2,1)}, bf16[1024,1024]{1,0:T(8,128)(2,1)}, u32[]{:S(2)}, u32[]{:S(2)}) collective-permute-start(bf16[1024,1024]{1,0:T(8,128)(2,1)} %constant_dynamic-slice_fusion.2), channel_id=1, source_target_pairs={{0,2},{2,0},{4,6},{6,4},{8,10},{10,8},{12,14},{14,12},{16,18},{18,... | collective-permute-start | bytes 6291464 | tf_op jit(solution)/shard_map/ppermute | solution.py:398
  246.3 173.1 %collective-permute-start.18 = (bf16[1024,1024]{1,0:T(8,128)(2,1)}, bf16[1024,1024]{1,0:T(8,128)(2,1)}, u32[]{:S(2)}, u32[]{:S(2)}) collective-permute-start(bf16[1024,1024]{1,0:T(8,128)(2,1)} %constant_dynamic-slice_fusion.1), channel_id=1, source_target_pairs={{0,2},{2,0},{4,6},{6,4},{8,10},{10,8},{12,14},{14,12},{16,18},{18,... | collective-permute-start | bytes 6291464 | tf_op jit(solution)/shard_map/ppermute | solution.py:398
  308.3 41.4 %copy-start.30 = (bf16[512,1024]{1,0:T(8,128)(2,1)}, bf16[512,1024]{1,0:T(8,128)(2,1)S(1)}, u32[]{:S(2)}) copy-start(bf16[512,1024]{1,0:T(8,128)(2,1)S(1)} %convolution_convert_fusion.4) | copy-start | bytes 3145732
  313.2 37.3 %copy-start.14 = (bf16[1024,2048]{1,0:T(8,128)(2,1)}, bf16[1024,2048]{1,0:T(8,128)(2,1)S(1)}, u32[]{:S(2)}) copy-start(bf16[1024,2048]{1,0:T(8,128)(2,1)S(1)} %convolution_convert_fusion.2) | copy-start | bytes 12582916
  313.2 31.0 %copy-start.25 = (bf16[1024,1024]{0,1:T(8,128)(2,1)S(1)}, bf16[1024,1024]{0,1:T(8,128)(2,1)}, u32[]{:S(2)}) copy-start(bf16[1024,1024]{0,1:T(8,128)(2,1)} %fusion.17) | copy-start | bytes 6291460
  344.2 63.6 %copy-start.2 = (bf16[1024,512]{1,0:T(8,128)(2,1)}, bf16[1024,512]{1,0:T(8,128)(2,1)S(1)}, u32[]{:S(2)}) copy-start(bf16[1024,512]{1,0:T(8,128)(2,1)S(1)} %get-tuple-element.49) | copy-start | bytes 3145732
  349.6 216.2 %collective-permute-start.10 = (bf16[3,1024,256]{2,1,0:T(8,128)(2,1)}, bf16[3,1024,256]{2,1,0:T(8,128)(2,1)}, u32[]{:S(2)}, u32[]{:S(2)}) collective-permute-start(bf16[3,1024,256]{2,1,0:T(8,128)(2,1)} %slice.199), channel_id=1, source_target_pairs={{0,2},{2,0},{4,6},{6,4},{8,10},{10,8},{12,14},{14,12},{16,18},{18,... | collective-permute-start | bytes 4718600 | tf_op jit(solution)/shard_map/ppermute | solution.py:398
  352.1 64.3 %collective-permute-start.16 = (bf16[1024,1024]{1,0:T(8,128)(2,1)}, bf16[1024,1024]{1,0:T(8,128)(2,1)S(1)}, u32[]{:S(2)}, u32[]{:S(2)}) collective-permute-start(bf16[1024,1024]{1,0:T(8,128)(2,1)} %slice.203), channel_id=1, source_target_pairs={{0,2},{2,0},{4,6},{6,4},{8,10},{10,8},{12,14},{14,12},{16,18},{18,... | collective-permute-start | bytes 6291464 | tf_op jit(solution)/shard_map/ppermute | solution.py:398
  360.6 43.8 %collective-permute-start.19 = (bf16[1024,1024]{1,0:T(8,128)(2,1)}, bf16[1024,1024]{1,0:T(8,128)(2,1)}, u32[]{:S(2)}, u32[]{:S(2)}) collective-permute-start(bf16[1024,1024]{1,0:T(8,128)(2,1)} %slice.205), channel_id=1, source_target_pairs={{0,2},{2,0},{4,6},{6,4},{8,10},{10,8},{12,14},{14,12},{16,18},{18,... | collective-permute-start | bytes 6291464 | tf_op jit(solution)/shard_map/ppermute | solution.py:398
  361.7 30.7 %copy-start.26 = (bf16[1024,1024]{0,1:T(8,128)(2,1)S(1)}, bf16[1024,1024]{0,1:T(8,128)(2,1)}, u32[]{:S(2)}) copy-start(bf16[1024,1024]{0,1:T(8,128)(2,1)} %fusion.17) | copy-start | bytes 6291460
  407.9 47.6 %collective-permute-start.20 = (bf16[1024,1024]{1,0:T(8,128)(2,1)}, bf16[1024,1024]{1,0:T(8,128)(2,1)}, u32[]{:S(2)}, u32[]{:S(2)}) collective-permute-start(bf16[1024,1024]{1,0:T(8,128)(2,1)} %slice_add_fusion), channel_id=1, source_target_pairs={{0,1},{1,0},{2,3},{3,2},{4,5},{5,4},{6,7},{7,6},{8,9},{9,8},{10,11... | collective-permute-start | bytes 6291464 | tf_op jit(solution)/shard_map/ppermute | solution.py:393
  416.3 39.2 %copy-start.22 = (bf16[2048,1024]{1,0:T(8,128)(2,1)S(1)}, bf16[2048,1024]{1,0:T(8,128)(2,1)}, u32[]{:S(2)}) copy-start(bf16[2048,1024]{1,0:T(8,128)(2,1)} %copy-done.21) | copy-start | bytes 12582916
  416.4 253.6 %collective-permute-start.9 = (bf16[3,1024,256]{2,1,0:T(8,128)(2,1)}, bf16[3,1024,256]{2,1,0:T(8,128)(2,1)}, u32[]{:S(2)}, u32[]{:S(2)}) collective-permute-start(bf16[3,1024,256]{2,1,0:T(8,128)(2,1)} %constant_dynamic-slice_fusion.4), channel_id=1, source_target_pairs={{0,2},{2,0},{4,6},{6,4},{8,10},{10,8},{12,14},{14,12},{16,18},{18,... | collective-permute-start | bytes 4718600 | tf_op jit(solution)/shard_map/ppermute | solution.py:398
  419.4 41.2 %copy-start.64 = (f32[1024]{0:T(1024)S(1)}, f32[1024]{0:T(1024)}, u32[]{:S(2)}) copy-start(f32[1024]{0:T(1024)} %param.29) | copy-start | bytes 12292
  419.4 150.9 %collective-permute-start.13 = (bf16[256,1024]{1,0:T(8,128)(2,1)}, bf16[256,1024]{1,0:T(8,128)(2,1)}, u32[]{:S(2)}, u32[]{:S(2)}) collective-permute-start(bf16[256,1024]{1,0:T(8,128)(2,1)} %slice.201), channel_id=1, source_target_pairs={{0,2},{2,0},{4,6},{6,4},{8,10},{10,8},{12,14},{14,12},{16,18},{18,... | collective-permute-start | bytes 1572872 | tf_op jit(solution)/shard_map/ppermute | solution.py:398
  455.5 46.8 %collective-permute-start.17 = (bf16[1024,1024]{1,0:T(8,128)(2,1)}, bf16[1024,1024]{1,0:T(8,128)(2,1)}, u32[]{:S(2)}, u32[]{:S(2)}) collective-permute-start(bf16[1024,1024]{1,0:T(8,128)(2,1)} %slice_add_fusion.1), channel_id=1, source_target_pairs={{0,1},{1,0},{2,3},{3,2},{4,5},{5,4},{6,7},{7,6},{8,9},{9,8},{10,11... | collective-permute-start | bytes 6291464 | tf_op jit(solution)/shard_map/ppermute | solution.py:393
  460.6 209.3 %all-reduce.7.cloned.1.call-start = ((), (), s32[]{:S(2)}) async-start(), calls=%async_computation.1 | async-start | bytes 4194304 | tf_op jit(solution)/shard_map/psum | solution.py:420
  483.5 80.6 %copy-start.53 = (f32[1024]{0:T(1024)S(1)}, f32[1024]{0:T(1024)}, u32[]{:S(2)}) copy-start(f32[1024]{0:T(1024)} %get-tuple-element.98) | copy-start | bytes 12292
  483.5 90.2 %collective-permute-start.12 = (bf16[256,1024]{1,0:T(8,128)(2,1)}, bf16[256,1024]{1,0:T(8,128)(2,1)}, u32[]{:S(2)}, u32[]{:S(2)}) collective-permute-start(bf16[256,1024]{1,0:T(8,128)(2,1)} %constant_dynamic-slice_fusion.3), channel_id=1, source_target_pairs={{0,2},{2,0},{4,6},{6,4},{8,10},{10,8},{12,14},{14,12},{16,18},{18,... | collective-permute-start | bytes 1572872 | tf_op jit(solution)/shard_map/ppermute | solution.py:398
  507.3 63.0 %copy-start.61 = (f32[1024]{0:T(1024)S(1)}, f32[1024]{0:T(1024)}, u32[]{:S(2)}) copy-start(f32[1024]{0:T(1024)} %get-tuple-element.88) | copy-start | bytes 12292
  507.3 63.0 %copy-start.60 = (f32[1024]{0:T(1024)S(1)}, f32[1024]{0:T(1024)}, u32[]{:S(2)}) copy-start(f32[1024]{0:T(1024)} %get-tuple-element.92) | copy-start | bytes 12292
  564.1 180.3 %all-reduce.9.cloned.1.call-start = ((), (), s32[]{:S(2)}) async-start(), calls=%async_computation.2 | async-start | bytes 1048576 | tf_op jit(solution)/shard_map/psum | solution.py:420
  565.8 49.7 %copy-start.33 = (bf16[512,1024]{1,0:T(8,128)(2,1)S(1)}, bf16[512,1024]{1,0:T(8,128)(2,1)}, u32[]{:S(2)}) copy-start(bf16[512,1024]{1,0:T(8,128)(2,1)} %copy-done.32) | copy-start | bytes 3145732
  569.1 100.8 %copy-start.43 = (f32[2048]{0:T(1024)S(1)}, f32[2048]{0:T(1024)}, u32[]{:S(2)}) copy-start(f32[2048]{0:T(1024)} %get-tuple-element.151) | copy-start | bytes 24580
  569.1 100.9 %collective-permute-start.11 = (bf16[3,1024,256]{2,1,0:T(8,128)(2,1)}, bf16[3,1024,256]{2,1,0:T(8,128)(2,1)}, u32[]{:S(2)}, u32[]{:S(2)}) collective-permute-start(bf16[3,1024,256]{2,1,0:T(8,128)(2,1)} %slice_add_fusion.2), channel_id=1, source_target_pairs={{0,1},{1,0},{2,3},{3,2},{4,5},{5,4},{6,7},{7,6},{8,9},{9,8},{10,11... | collective-permute-start | bytes 4718600 | tf_op jit(solution)/shard_map/ppermute | solution.py:393
  571.5 44.1 %collective-permute-start.14 = (bf16[256,1024]{1,0:T(8,128)(2,1)S(1)}, bf16[256,1024]{1,0:T(8,128)(2,1)S(1)}, u32[]{:S(2)}, u32[]{:S(2)}) collective-permute-start(bf16[256,1024]{1,0:T(8,128)(2,1)S(1)} %slice_add_fusion.3), channel_id=1, source_target_pairs={{0,1},{1,0},{2,3},{3,2},{4,5},{5,4},{6,7},{7,6},{8,9},{9,8},{10,11... | collective-permute-start | bytes 1572872 | tf_op jit(solution)/shard_map/ppermute | solution.py:393
  572.2 227.3 %collective-permute-start.24 = (bf16[1024,1024]{1,0:T(8,128)(2,1)}, bf16[1024,1024]{1,0:T(8,128)(2,1)}, u32[]{:S(2)}, u32[]{:S(2)}) collective-permute-start(bf16[1024,1024]{1,0:T(8,128)(2,1)} %all-reduce.5.cloned.1.call-done), channel_id=1, source_target_pairs={{0,2},{2,0},{4,6},{6,4},{8,10},{10,8},{12,14},{14,12},{16,18},{18,... | collective-permute-start | bytes 6291464 | tf_op jit(solution)/shard_map/ppermute | solution.py:398
  617.6 129.4 %copy-start.50 = (f32[2048]{0:T(1024)S(1)}, f32[2048]{0:T(1024)}, u32[]{:S(2)}) copy-start(f32[2048]{0:T(1024)} %get-tuple-element.149) | copy-start | bytes 24580
  669.9 118.8 %copy-start.27 = (bf16[1024,1024]{0,1:T(8,128)(2,1)S(1)}, bf16[1024,1024]{0,1:T(8,128)(2,1)}, u32[]{:S(2)}) copy-start(bf16[1024,1024]{0,1:T(8,128)(2,1)} %get-tuple-element.109) | copy-start | bytes 6291460
  669.9 170.6 %all-reduce.11.cloned.1.call-start = ((), (), s32[]{:S(2)}) async-start(), calls=%async_computation.3 | async-start | bytes 3145728 | tf_op jit(solution)/shard_map/psum | solution.py:420
  744.5 105.5 %collective-permute-start.23 = (bf16[1024,1024]{1,0:T(8,128)(2,1)}, bf16[1024,1024]{1,0:T(8,128)(2,1)}, u32[]{:S(2)}, u32[]{:S(2)}) collective-permute-start(bf16[1024,1024]{1,0:T(8,128)(2,1)} %all-reduce.7.cloned.1.call-done), channel_id=1, source_target_pairs={{0,2},{2,0},{4,6},{6,4},{8,10},{10,8},{12,14},{14,12},{16,18},{18,... | collective-permute-start | bytes 6291464 | tf_op jit(solution)/shard_map/ppermute | solution.py:398
  798.5 48.6 %collective-permute-start.22 = (bf16[256,1024]{1,0:T(8,128)(2,1)S(1)}, bf16[256,1024]{1,0:T(8,128)(2,1)}, u32[]{:S(2)}, u32[]{:S(2)}) collective-permute-start(bf16[256,1024]{1,0:T(8,128)(2,1)S(1)} %copy-done.39), channel_id=1, source_target_pairs={{0,2},{2,0},{4,6},{6,4},{8,10},{10,8},{12,14},{14,12},{16,18},{18,... | collective-permute-start | bytes 1572872 | tf_op jit(solution)/shard_map/ppermute | solution.py:398
  840.5 16.0 %collective-permute-start.21 = (bf16[3,1024,256]{2,1,0:T(8,128)(2,1)}, bf16[3,1024,256]{2,1,0:T(8,128)(2,1)S(1)}, u32[]{:S(2)}, u32[]{:S(2)}) collective-permute-start(bf16[3,1024,256]{2,1,0:T(8,128)(2,1)} %all-reduce.11.cloned.1.call-done), channel_id=1, source_target_pairs={{0,2},{2,0},{4,6},{6,4},{8,10},{10,8},{12,14},{14,12},{16,18},{18,... | collective-permute-start | bytes 4718600 | tf_op jit(solution)/shard_map/ppermute | solution.py:398
  (50 other events, 264.3 us)
Sparse Core Ops, SparseCore 0:
  460.7 103.3 all-reduce.4
  568.2 101.5 all-reduce.6
  673.8 70.5 all-reduce.8
  748.8 91.6 all-reduce.10

commit v2 on v1

--- a/solution.py
+++ b/solution.py
@@ -296,8 +296,9 @@
 
 
 def pair_backward(
-    query_ref, keys_ref, values_ref, grad_ref, logs_ref, dq_ref, dk_ref, dv_ref, dk_sum, dv_sum
+    query_ref, keys_ref, values_ref, grad_ref, logs_ref, *others
 ):
+    dq_ref, dk_ref, dv_ref, dk_sum, dv_sum = others[-5:]
     keys = keys_ref[...]
     values = values_ref[...]
     grad = grad_ref[...]
@@ -365,7 +366,7 @@
     )(projected, projected, projected)
 
 
-def attend_grad(projected, grad_mixed, logs):
+def attend_grad(projected, grad_mixed, logs, earlier):
     rows, columns = grad_mixed.shape
     pairs, images = columns // PAIR, rows // SEQ
     area = images * columns // HD * SEQ * SEQ
@@ -378,7 +379,8 @@
             part_spec(2 * pairs),
             part_spec(0),
             logs_spec(pairs),
-        ],
+        ]
+        + [pl.BlockSpec(memory_space=pl.ANY)] * len(earlier),
         out_specs=[part_spec(0)] * 3,
         out_shape=[jax.ShapeDtypeStruct((rows, columns), jnp.bfloat16)] * 3,
         scratch_shapes=[pltpu.VMEM((SEQ, PAIR), jnp.float32)] * 2,
@@ -386,7 +388,7 @@
         cost_estimate=pl.CostEstimate(
             flops=40 * area * HD, bytes_accessed=14 * rows * columns, transcendentals=area
         ),
-    )(projected, projected, projected, grad_mixed, logs)
+    )(projected, projected, projected, grad_mixed, logs, *earlier)
 
 
 def over_group(values):
@@ -398,13 +400,14 @@
     return lax.ppermute(values, "dp", [(index, index ^ 1) for index in range(size)])
 
 
-def fetch(weight, axis, parity):
+def fetch(weight, axis, parity, earlier):
     half = weight.shape[axis] // 2
     near = over_group(lax.dynamic_slice_in_dim(weight, parity * half, half, axis))
+    near, _ = lax.optimization_barrier((near, earlier))
     return jnp.concatenate([near, over_pair(near)], axis=axis)
 
 
-def sum_everywhere(own, other, axis, parity, after):
+def sum_four(own, other, axis, parity):
     half = own.shape[axis] // 2
     keep = lax.dynamic_slice_in_dim(own, parity * half, half, axis)
     give = lax.dynamic_slice_in_dim(own, (1 - parity) * half, half, axis)
@@ -412,7 +415,10 @@
     other_give = lax.slice_in_dim(other, half, 2 * half, axis=axis)
     other_sum = other_keep + over_pair(other_give)
     own_sum = keep + over_pair(give)
-    quarter = own_sum + over_group(other_sum)
+    return own_sum + over_group(other_sum)
+
+
+def sum_parity(quarter, after):
     if after is not None:
         quarter, after = lax.optimization_barrier((quarter, after))
     size = lax.axis_size("dp")
@@ -473,15 +479,9 @@
     biases = over_group(jnp.concatenate([qv_bias.reshape(-1), up_bias]))
     qv_other = in_order(biases[: 2 * columns].reshape(2, columns))
     up_bias_other = in_order(biases[2 * columns :])
-    out_other = fetch(out_weight, 0, parity)
-    up_other = fetch(up_weight, 1, parity)
-    down_other = fetch(down_weight, 0, parity)
     qkv_pair = (qkv_own, qkv_other)
     qv_pair = (qv_bias, qv_other)
-    out_pair = (out_weight, out_other)
-    up_pair = (up_weight, up_other)
     up_bias_pair = (up_bias, up_bias_other)
-    down_pair = (down_weight, down_other)
 
     residual = tokens.astype(jnp.float32)
     first_norm = norm_rows(residual, first_gain, first_bias).astype(low)
@@ -494,6 +494,9 @@
         part, log_part = attend(projected[-1])
         mixed.append(part)
         logs.append(log_part)
+    out_pair = (out_weight, fetch(out_weight, 0, parity, mixed[0]))
+    up_pair = (up_weight, fetch(up_weight, 1, parity, mixed[1]))
+    down_pair = (down_weight, fetch(down_weight, 0, parity, mixed[1]))
     attention = contract(mixed[0], out_pair[0]) + contract(mixed[1], out_pair[1]) + out_bias
     after_attention = residual + attention_scale * attention
     second_norm = norm_rows(after_attention, second_gain, second_bias).astype(low)
@@ -513,17 +516,19 @@
     grad_mlp_scale = jnp.sum(upstream * feed, axis=0)
     grad_feed = (upstream * mlp_scale).astype(low)
     grad_down_bias = jnp.sum(grad_feed.astype(jnp.float32), axis=0)
-    down_sum, _ = sum_everywhere(
-        *[contract_first(act, grad_feed).astype(low) for act in hidden], 0, parity, None
-    )
+    down_quarter = sum_four(
+        *[contract_first(act, grad_feed).astype(low) for act in hidden], 0, parity
+    )
+    down_sum, _ = sum_parity(down_quarter, None)
     grad_pre = [
         (contract_last(grad_feed, weight) * slope.astype(jnp.float32)).astype(low)
         for weight, slope in zip(down_pair, slopes)
     ]
     grad_up_bias = [jnp.sum(part.astype(jnp.float32), axis=0) for part in grad_pre]
-    up_sum, down_sum = sum_everywhere(
-        *[contract_first(second_norm, part).astype(low) for part in grad_pre], 1, parity, down_sum
-    )
+    up_quarter = sum_four(
+        *[contract_first(second_norm, part).astype(low) for part in grad_pre], 1, parity
+    )
+    up_sum, down_sum = sum_parity(up_quarter, down_sum)
     grad_second = contract_last(grad_pre[0], up_pair[0]) + contract_last(grad_pre[1], up_pair[1])
     _, second_pull = jax.vjp(norm_rows, after_attention, second_gain, second_bias)
     grad_after, grad_second_gain, grad_second_bias = second_pull(grad_second)
@@ -531,21 +536,23 @@
     grad_attention_scale = jnp.sum(grad_after * attention, axis=0)
     grad_attention = (grad_after * attention_scale).astype(low)
     grad_out_bias = jnp.sum(grad_attention.astype(jnp.float32), axis=0)
-    out_sum, up_sum = sum_everywhere(
-        *[contract_first(part, grad_attention).astype(low) for part in mixed], 0, parity, up_sum
-    )
+    out_quarter = sum_four(
+        *[contract_first(part, grad_attention).astype(low) for part in mixed], 0, parity
+    )
+    out_sum, up_sum = sum_parity(out_quarter, up_sum)
+    earlier = ([down_quarter], [up_quarter, out_quarter, down_sum])
     grad_projected = []
     grad_qv = []
     qkv_grads = []
-    for part, log_part, weight in zip(projected, logs, out_pair):
+    for part, log_part, weight, ready in zip(projected, logs, out_pair, earlier):
         grad_mixed = contract_last(grad_attention, weight).astype(low)
-        parts = attend_grad(part, grad_mixed, log_part)
+        parts = attend_grad(part, grad_mixed, log_part, ready)
         grad_qv.append(
             jnp.stack([jnp.sum(parts[j].astype(jnp.float32), axis=0) for j in (0, 2)])
         )
         grad_projected.append(jnp.concatenate(parts, axis=1))
         qkv_grads.append(jnp.stack([contract_first(first_norm, each).astype(low) for each in parts]))
-    qkv_sum, out_sum = sum_everywhere(*qkv_grads, 2, parity, out_sum)
+    qkv_sum, out_sum = sum_parity(sum_four(*qkv_grads, 2, parity), out_sum)
     grad_first = contract_last(grad_projected[0], qkv_pair[0]) + contract_last(
         grad_projected[1], qkv_pair[1]
     )

time: 874 us -> 890 us (1.018)
  waiting for transfers between devices: 388 us -> 412 us
    psum x4, waiting for transfers between devices: 216 us -> 257 us  [sum_parity(): return (lax.psum(quarter, 'dp', axis_index_groups=groups), after)]
    ppermute x9, waiting for transfers between devices: 171 us -> 154 us  [over_group(): return lax.ppermute(values, 'tensor', [(0, 1), (1, 0)])]
    unnamed x160 -> x142, local copies, waits for them, and re-layouts: 51.4 us -> 49.3 us
  transfers between devices with their start and end apart: 29 -> 29, of which waited for: 10 -> 6; matrix products, arithmetic and copies ran while one was open for 30% -> 29% of each run, Pallas kernels for 13% -> 13%
where the time goes in v2:
time: 890 us; the launch traced here: 880 us
  waiting for transfers between devices  412 us (46%)
  matrix products  155 us (17%)
  Pallas kernels  111 us (12%)
  local copies, waits for them, and re-layouts  69 us (8%)
  other arithmetic  56.6 us (6%)
  blocking collectives  41.7 us (5%)
  starting transfers between devices  18.9 us (2%)
  between operations  15.4 us (2%)
    psum x4, waiting for transfers between devices, sum_parity(): return (lax.psum(quarter, 'dp', axis_index_groups=groups), after)  257 us
    ppermute x9, waiting for transfers between devices, over_group(): return lax.ppermute(values, 'tensor', [(0, 1), (1, 0)])  154 us
    dot_general x8, matrix products, contract(): return jnp.dot(left, right, preferred_element_type=jnp.float32)  62.4 us
    pallas_call x2, Pallas kernels, attend_grad(): pl.pallas_call(pair_backward, grid=(images, pairs), in_specs=[part_spec(0...  60.9 us
    dot_general x8, matrix products, contract_last(): lax.dot_general(left, right, (((1,), (1,)), ((), ())), preferred_element_...  55.8 us
    pallas_call x2, Pallas kernels, attend(): pl.pallas_call(pair_forward, grid=(images, pairs), in_specs=[part_spec(0)...  49.8 us
    unnamed x142, local copies, waits for them, and re-layouts  49.3 us
    psum x1, blocking collectives, image_body(): lax.psum(jnp.concatenate([grad_first_gain, grad_first_bias, grad_out_bias...  41.7 us
  transfers between devices with their start and end apart: 29, of which 6 were waited for; matrix products, arithmetic and copies ran while one was open for 29% of the time, Pallas kernels for 13%

profile of v2, /device:TPU:1, one launch (start us, length us, event | category | flops | bytes accessed | tf_op | source)
XLA Modules:
  0.0 879.9 jit_solution(11984680291231356628)
XLA Ops:
  11.6 3.2 constant_dynamic-slice_fusion.5
  17.8 4.7 copy.43
  26.7 2.9 copy.42
  33.3 3.9 copy.46
  37.3 6.0 add_convert_fusion.1.query_ref.keys_ref.values_ref
  43.3 104.6 %collective-permute-done = bf16[1024,768]{0,1:T(8,128)(2,1)} collective-permute-done((bf16[1024,768]{0,1:T(8,128)(2,1)}, bf16[1024,768]{0,1:T(8,128)(2,1)}, u32[]{:S(2)}, u32[]{:S(2)}) %collective-permute-start) | collective-permute-done | bytes 1572896 | tf_op jit(solution)/shard_map/ppermute | solution.py:395
  149.8 25.0 %shard_map.279 = (bf16[1024,512]{1,0:T(8,128)(2,1)S(1)}, f32[4,2,1024]{2,1,0:T(2,128)S(1)}) custom-call(bf16[1024,1536]{1,0:T(8,128)(2,1)S(1)} %add_convert_fusion.1.query_ref.keys_ref.values_ref, bf16[1024,1536]{1,0:T(8,128)(2,1)S(1)} %add_convert_fusion.1.query_ref.keys_ref.values_ref, bf16[1024,1536]{1,0:T(8,128)(2,1)S(1)} %add_convert_fusion.1.query_ref.keys_ref.values_ref), custom_call_target="tpu_custom_call" | custom-call | flops 8589934592 | bytes 4194304 | tf_op jit(solution)/shard_map/pallas_call | solution.py:353
  186.1 3.8 add_convert_fusion.query_ref.keys_ref.values_ref
  189.9 24.8 %shard_map.280 = (bf16[1024,512]{1,0:T(8,128)(2,1)S(1)}, f32[4,2,1024]{2,1,0:T(2,128)S(1)}) custom-call(bf16[1024,1536]{1,0:T(8,128)(2,1)S(1)} %add_convert_fusion.query_ref.keys_ref.values_ref, bf16[1024,1536]{1,0:T(8,128)(2,1)S(1)} %add_convert_fusion.query_ref.keys_ref.values_ref, bf16[1024,1536]{1,0:T(8,128)(2,1)S(1)} %add_convert_fusion.query_ref.keys_ref.values_ref), custom_call_target="tpu_custom_call" | custom-call | flops 8589934592 | bytes 4194304 | tf_op jit(solution)/shard_map/pallas_call | solution.py:353
  215.4 3.3 fusion.60
  222.3 9.7 %fusion.4 = (bf16[1024,2048]{1,0:T(8,128)(2,1)}, bf16[1024,2048]{1,0:T(8,128)(2,1)}) fusion(f32[2048]{0:T(1024)S(1)} %copy-done.51, bf16[1024,1024]{0,1:T(8,128)(2,1)S(1)} %add_convert_fusion.3, bf16[1024,2048]{1,0:T(8,128)(2,1)S(1)} %copy-done.31), kind=kOutput, calls=%fused_computation.6 | convolution fusion | flops 4320133120 | bytes 14688256 | tf_op jit(solution)/shard_map/dot_general | solution.py:264
  232.0 10.1 %convert_reduce_fusion.1 = (f32[2048]{0:T(1024)}, bf16[1024,2048]{1,0:T(8,128)(2,1)}) fusion(bf16[1024,2048]{1,0:T(8,128)(2,1)} %get-tuple-element.46, bf16[2048,1024]{1,0:T(8,128)(2,1)} %param.28, bf16[1024,1024]{0,1:T(8,128)(2,1)S(1)} %copy-done.15, f32[1024]{0:T(1024)S(1)} %copy-done.55), kind=kOutput, calls=%fused_computation.13 | convolution fusion | flops 4308596736 | bytes 14692352 | tf_op jit(solution)/shard_map/dot_general | solution.py:268
  242.1 8.4 fusion.69
  250.5 5.6 convolution_convert_fusion.3
  256.1 4.9 convolution_convert_fusion.1
  261.0 11.5 %fusion.68 = f32[1024,1024]{0,1:T(8,128)} fusion(bf16[1024,2048]{1,0:T(8,128)(2,1)} %get-tuple-element.42, bf16[2048,1024]{1,0:T(8,128)(2,1)} %param.28), kind=kOutput, calls=%fused_computation.193 | convolution fusion | flops 4294967296 | bytes 12582912 | tf_op jit(solution)/shard_map/dot_general | solution.py:264
  281.6 9.4 %fusion.9 = (bf16[1024,2048]{1,0:T(8,128)(2,1)}, bf16[1024,2048]{1,0:T(8,128)(2,1)}) fusion(f32[2048]{0:T(1024)S(1)} %slice_select_fusion, bf16[1024,1024]{0,1:T(8,128)(2,1)S(1)} %add_convert_fusion.3, bf16[1024,2048]{1,0:T(8,128)(2,1)S(1)} %constant_dynamic-update-slice_fusion.2), kind=kOutput, calls=%fused_computation.11 | convolution fusion | flops 4320133120 | bytes 14688256 | tf_op jit(solution)/shard_map/dot_general | solution.py:264
  291.1 9.7 %convert_reduce_fusion = (f32[2048]{0:T(1024)S(1)}, bf16[1024,2048]{1,0:T(8,128)(2,1)}) fusion(bf16[1024,2048]{1,0:T(8,128)(2,1)} %get-tuple-element.47, bf16[2048,1024]{1,0:T(8,128)(2,1)S(1)} %constant_dynamic-update-slice_fusion.4, bf16[1024,1024]{0,1:T(8,128)(2,1)S(1)} %copy-done.15, f32[1024]{0:T(1024)S(1)} %copy-done.55), kind=kOutput, calls=%fused_computation.12 | convolution fusion | flops 4308596736 | bytes 14692352 | tf_op jit(solution)/shard_map/dot_general | solution.py:268
  300.8 7.1 convolution_convert_fusion
  309.6 2.7 copy-done.59
  312.4 5.6 convolution_convert_fusion.2
  320.9 8.9 %multiply_reduce_fusion = (f32[1024]{0:T(1024)S(1)}, f32[1024]{0:T(1024)S(1)}, f32[1024]{0:T(1024)S(1)}, f32[1024,1024]{0,1:T(8,128)S(1)}) fusion(f32[1024,1024]{0,1:T(8,128)S(1)} %get-tuple-element.109, f32[1024]{0:T(1024)S(1)} %fusion.49, f32[1024]{0:T(1024)S(1)} %broadcast_multiply_fusion, f32[1024]{0:T(1024)S(1)} %copy-done.46, ...), kind=kOutput, calls=%fused_computation.47 | convolution fusion | flops 4304401408 | bytes 20996096 | tf_op jit(solution)/shard_map/dot_general | solution.py:268
  338.3 2.3 convolution_convert_fusion.12.grad_ref
  342.1 2.3 convolution_convert_fusion.13.grad_ref
  344.7 49.6 %collective-permute-done.17 = bf16[256,1024]{1,0:T(8,128)(2,1)S(1)} collective-permute-done((bf16[256,1024]{1,0:T(8,128)(2,1)S(1)}, bf16[256,1024]{1,0:T(8,128)(2,1)S(1)}, u32[]{:S(2)}, u32[]{:S(2)}) %collective-permute-start.17) | collective-permute-done | bytes 524320 | tf_op jit(solution)/shard_map/ppermute | solution.py:395
  394.6 3.3 slice_add_fusion
  398.1 5.1 add_add_fusion.6.others_0_
  404.4 30.6 %shard_map.281 = (bf16[1024,512]{1,0:T(8,128)(2,1)S(1)}, bf16[1024,512]{1,0:T(8,128)(2,1)S(1)}, bf16[1024,512]{1,0:T(8,128)(2,1)S(1)}) custom-call(bf16[1024,1536]{1,0:T(8,128)(2,1)} %copy-done.9, bf16[1024,1536]{1,0:T(8,128)(2,1)} %copy-done.9, bf16[1024,1536]{1,0:T(8,128)(2,1)} %copy-done.9, bf16[1024,512]{1,0:T(8,128)(2,1)S(1)} %copy-done.4, ...), custom_call_target="tpu_custom_call" | custom-call | flops 21474836480 | bytes 7340032 | tf_op jit(solution)/shard_map/pallas_call | solution.py:373
  436.7 3.2 fusion.39
  447.6 5.6 add_add_fusion.5.others_0_
  453.2 7.7 fusion.23
  460.9 83.3 %all-reduce.5.cloned.1.call-done.others_2_ = bf16[1024,1024]{1,0:T(8,128)(2,1)} async-done(((bf16[1024,1024]{1,0:T(8,128)(2,1)}), bf16[1024,1024]{1,0:T(8,128)(2,1)}) %all-reduce.5.cloned.1.call-update) | async-done | bytes 2097168 | tf_op jit(solution)/shard_map/psum | solution.py:426
  546.3 30.3 %shard_map.282 = (bf16[1024,512]{1,0:T(8,128)(2,1)S(1)}, bf16[1024,512]{1,0:T(8,128)(2,1)S(1)}, bf16[1024,512]{1,0:T(8,128)(2,1)S(1)}) custom-call(bf16[1024,1536]{1,0:T(8,128)(2,1)} %copy-done.8, bf16[1024,1536]{1,0:T(8,128)(2,1)} %copy-done.8, bf16[1024,1536]{1,0:T(8,128)(2,1)} %copy-done.8, bf16[1024,512]{1,0:T(8,128)(2,1)S(1)} %copy-done.3, ...), custom_call_target="tpu_custom_call" | custom-call | flops 21474836480 | bytes 7340032 | tf_op jit(solution)/shard_map/pallas_call | solution.py:373
  578.5 3.2 fusion.42
  587.1 6.3 fusion.58
  598.3 17.5 %fusion.22 = (f32[1024]{0:T(1024)S(1)}, f32[1024]{0:T(1024)S(1)}, f32[1024]{0:T(1024)S(1)}, f32[1024,1024]{0,1:T(8,128)}, bf16[1024,1024]{0,1:T(8,128)(2,1)}) fusion(bf16[1024,1024]{0,1:T(8,128)(2,1)} %copy.46, f32[1024]{0:T(1024)S(1)} %copy-done.55, f32[1024,1024]{0,1:T(8,128)} %get-tuple-element.152, f32[1024,1024]{0,1:T(8,128)} %copy-done.13, ...), kind=kOutput, calls=%fused_computation.43 | convolution fusion | flops 4321178624 | bytes 39890944 | tf_op jit(solution)/shard_map/dot_general | solution.py:264
  616.2 66.8 %all-reduce.7.cloned.1.call-done = bf16[1024,1024]{1,0:T(8,128)(2,1)} async-done(((bf16[1024,1024]{1,0:T(8,128)(2,1)}), bf16[1024,1024]{1,0:T(8,128)(2,1)}) %all-reduce.7.cloned.1.call-update) | async-done | bytes 2097168 | tf_op jit(solution)/shard_map/psum | solution.py:426
  683.1 4.2 add_add_fusion.7
  687.4 69.6 %all-reduce.9.cloned.1.call-done = bf16[256,1024]{1,0:T(8,128)(2,1)} async-done(((bf16[256,1024]{1,0:T(8,128)(2,1)}), bf16[256,1024]{1,0:T(8,128)(2,1)}) %all-reduce.9.cloned.1.call-update) | async-done | bytes 524304 | tf_op jit(solution)/shard_map/psum | solution.py:426
  757.0 2.6 collective-permute-start.23
  759.6 41.7 %psum.36 = f32[14336]{0:T(1024)S(1)} all-reduce(f32[14336]{0:T(1024)S(1)} %select_dynamic-update-slice_fusion), channel_id=1, replica_groups=mesh['dp'=16,'tensor'=2] {'dp','tensor'}, use_global_device_ids=true, to_apply=%region_23.24 | all-reduce | flops 14336 | bytes 114688 | tf_op jit(solution)/shard_map/psum | solution.py:571
  801.3 2.6 copy.51
  803.9 5.4 copy.52
  812.0 3.9 broadcast_select_fusion.1
  815.9 37.2 %all-reduce.11.cloned.1.call-done = bf16[3,1024,256]{2,1,0:T(8,128)(2,1)} async-done(((bf16[3,1024,256]{2,1,0:T(8,128)(2,1)}), bf16[3,1024,256]{2,1,0:T(8,128)(2,1)}) %all-reduce.11.cloned.1.call-update) | async-done | bytes 1572880 | tf_op jit(solution)/shard_map/psum | solution.py:426
  853.5 6.2 maximum_convert_fusion.1
  864.6 4.4 maximum_convert_fusion
  869.3 3.6 convert_bitcast_fusion
  (264 shorter events, 90.4 us)
Async XLA Ops:
  8.7 28.6 %collective-permute-start.2 = (f32[3072]{0:T(1024)S(1)}, f32[3072]{0:T(1024)S(1)}, u32[]{:S(2)}, u32[]{:S(2)}) collective-permute-start(f32[3072]{0:T(1024)S(1)} %pad_maximum_fusion.3), channel_id=1, source_target_pairs={{0,1},{1,0},{2,3},{3,2},{4,5},{5,4},{6,7},{7,6},{8,9},{9,8},{10,11... | collective-permute-start | bytes 36872 | tf_op jit(solution)/shard_map/ppermute | solution.py:395
  11.6 163.3 %collective-permute-start.3 = (bf16[256,1024]{1,0:T(8,128)(2,1)}, bf16[256,1024]{1,0:T(8,128)(2,1)}, u32[]{:S(2)}, u32[]{:S(2)}) collective-permute-start(bf16[256,1024]{1,0:T(8,128)(2,1)} %constant_dynamic-slice_fusion.7), channel_id=1, source_target_pairs={{0,1},{1,0},{2,3},{3,2},{4,5},{5,4},{6,7},{7,6},{8,9},{9,8},{10,11... | collective-permute-start | bytes 1572872 | tf_op jit(solution)/shard_map/ppermute | solution.py:395
  14.8 199.9 %collective-permute-start.7 = (bf16[1024,1024]{1,0:T(8,128)(2,1)}, bf16[1024,1024]{1,0:T(8,128)(2,1)}, u32[]{:S(2)}, u32[]{:S(2)}) collective-permute-start(bf16[1024,1024]{1,0:T(8,128)(2,1)} %constant_dynamic-slice_fusion.5), channel_id=1, source_target_pairs={{0,1},{1,0},{2,3},{3,2},{4,5},{5,4},{6,7},{7,6},{8,9},{9,8},{10,11... | collective-permute-start | bytes 6291464 | tf_op jit(solution)/shard_map/ppermute | solution.py:395
  17.8 196.9 %collective-permute-start.5 = (bf16[1024,1024]{1,0:T(8,128)(2,1)}, bf16[1024,1024]{1,0:T(8,128)(2,1)}, u32[]{:S(2)}, u32[]{:S(2)}) collective-permute-start(bf16[1024,1024]{1,0:T(8,128)(2,1)} %constant_dynamic-slice_fusion.6), channel_id=1, source_target_pairs={{0,1},{1,0},{2,3},{3,2},{4,5},{5,4},{6,7},{7,6},{8,9},{9,8},{10,11... | collective-permute-start | bytes 6291464 | tf_op jit(solution)/shard_map/ppermute | solution.py:395
  25.2 122.8 %collective-permute-start = (bf16[1024,768]{0,1:T(8,128)(2,1)}, bf16[1024,768]{0,1:T(8,128)(2,1)}, u32[]{:S(2)}, u32[]{:S(2)}) collective-permute-start(bf16[1024,768]{0,1:T(8,128)(2,1)} %pad_maximum_fusion.2), channel_id=1, source_target_pairs={{0,1},{1,0},{2,3},{3,2},{4,5},{5,4},{6,7},{7,6},{8,9},{9,8},{10,11... | collective-permute-start | bytes 4718600 | tf_op jit(solution)/shard_map/ppermute | solution.py:395
  29.5 185.8 %copy-start.10 = (bf16[1024,1024]{0,1:T(8,128)(2,1)}, bf16[1024,1024]{0,1:T(8,128)(2,1)S(1)}, u32[]{:S(2)}) copy-start(bf16[1024,1024]{0,1:T(8,128)(2,1)S(1)} %copy.42) | copy-start | bytes 6291460
  43.3 131.5 %copy-start.9 = (bf16[1024,1536]{1,0:T(8,128)(2,1)}, bf16[1024,1536]{1,0:T(8,128)(2,1)S(1)}, u32[]{:S(2)}) copy-start(bf16[1024,1536]{1,0:T(8,128)(2,1)S(1)} %add_convert_fusion.1.query_ref.keys_ref.values_ref) | copy-start | bytes 9437188
  148.0 31.1 %collective-permute-start.1 = (bf16[1024,768]{0,1:T(8,128)(2,1)}, bf16[1024,768]{0,1:T(8,128)(2,1)}, u32[]{:S(2)}, u32[]{:S(2)}) collective-permute-start(bf16[1024,768]{0,1:T(8,128)(2,1)} %collective-permute-done), channel_id=1, source_target_pairs={{0,2},{2,0},{4,6},{6,4},{8,10},{10,8},{12,14},{14,12},{16,18},{18,... | collective-permute-start | bytes 4718600 | tf_op jit(solution)/shard_map/ppermute | solution.py:400
  174.8 2.6 collective-permute-start.4
  176.2 9.8 %copy-start.24 = (bf16[1024,1024]{0,1:T(8,128)(2,1)S(1)}, bf16[1024,1024]{0,1:T(8,128)(2,1)}, u32[]{:S(2)}) copy-start(bf16[1024,1024]{0,1:T(8,128)(2,1)} %fusion.17) | copy-start | bytes 6291460
  177.5 37.8 %copy-start.22 = (bf16[512,1024]{1,0:T(8,128)(2,1)}, bf16[512,1024]{1,0:T(8,128)(2,1)S(1)}, u32[]{:S(2)}) copy-start(bf16[512,1024]{1,0:T(8,128)(2,1)S(1)} %constant_dynamic-update-slice_fusion) | copy-start | bytes 3145732
  189.8 24.9 %copy-start.8 = (bf16[1024,1536]{1,0:T(8,128)(2,1)}, bf16[1024,1536]{1,0:T(8,128)(2,1)S(1)}, u32[]{:S(2)}) copy-start(bf16[1024,1536]{1,0:T(8,128)(2,1)S(1)} %add_convert_fusion.query_ref.keys_ref.values_ref) | copy-start | bytes 9437188
  189.9 25.5 %copy-start.47 = (f32[1024]{0:T(1024)S(1)}, f32[1024]{0:T(1024)}, u32[]{:S(2)}) copy-start(f32[1024]{0:T(1024)} %param.23) | copy-start | bytes 12292
  189.9 25.5 %copy-start.52 = (f32[1024]{0:T(1024)S(1)}, f32[1024]{0:T(1024)}, u32[]{:S(2)}) copy-start(f32[1024]{0:T(1024)} %param.22) | copy-start | bytes 12292
  214.7 65.0 %collective-permute-start.6 = (bf16[1024,1024]{1,0:T(8,128)(2,1)}, bf16[1024,1024]{1,0:T(8,128)(2,1)}, u32[]{:S(2)}, u32[]{:S(2)}) collective-permute-start(bf16[1024,1024]{1,0:T(8,128)(2,1)} %collective-permute-done.5), channel_id=1, source_target_pairs={{0,2},{2,0},{4,6},{6,4},{8,10},{10,8},{12,14},{14,12},{16,18},{18,... | collective-permute-start | bytes 6291464 | tf_op jit(solution)/shard_map/ppermute | solution.py:400
  215.3 75.6 %collective-permute-start.8 = (bf16[1024,1024]{1,0:T(8,128)(2,1)}, bf16[1024,1024]{1,0:T(8,128)(2,1)S(1)}, u32[]{:S(2)}, u32[]{:S(2)}) collective-permute-start(bf16[1024,1024]{1,0:T(8,128)(2,1)} %collective-permute-done.7), channel_id=1, source_target_pairs={{0,2},{2,0},{4,6},{6,4},{8,10},{10,8},{12,14},{14,12},{16,18},{18,... | collective-permute-start | bytes 6291464 | tf_op jit(solution)/shard_map/ppermute | solution.py:400
  218.6 111.2 %copy-start.12 = (f32[1024,1024]{0,1:T(8,128)}, f32[1024,1024]{0,1:T(8,128)S(1)}, u32[]{:S(2)}) copy-start(f32[1024,1024]{0,1:T(8,128)S(1)} %get-tuple-element.109) | copy-start | bytes 12582916
  222.3 9.7 %copy-start.15 = (bf16[1024,1024]{0,1:T(8,128)(2,1)S(1)}, bf16[1024,1024]{0,1:T(8,128)(2,1)}, u32[]{:S(2)}) copy-start(bf16[1024,1024]{0,1:T(8,128)(2,1)} %copy.46) | copy-start | bytes 6291460
  222.3 9.7 %copy-start.55 = (f32[1024]{0:T(1024)S(1)}, f32[1024]{0:T(1024)}, u32[]{:S(2)}) copy-start(f32[1024]{0:T(1024)} %param.30) | copy-start | bytes 12292
  256.1 16.5 %copy-start.20 = (bf16[2048,1024]{1,0:T(8,128)(2,1)}, bf16[2048,1024]{1,0:T(8,128)(2,1)S(1)}, u32[]{:S(2)}) copy-start(bf16[2048,1024]{1,0:T(8,128)(2,1)S(1)} %convolution_convert_fusion.3) | copy-start | bytes 12582916
  261.0 17.1 %copy-start.18 = (bf16[1024,2048]{1,0:T(8,128)(2,1)}, bf16[1024,2048]{1,0:T(8,128)(2,1)S(1)}, u32[]{:S(2)}) copy-start(bf16[1024,2048]{1,0:T(8,128)(2,1)S(1)} %convolution_convert_fusion.1) | copy-start | bytes 12582916
  274.1 124.0 %collective-permute-start.9 = (bf16[1024,1024]{1,0:T(8,128)(2,1)}, bf16[1024,1024]{1,0:T(8,128)(2,1)}, u32[]{:S(2)}, u32[]{:S(2)}) collective-permute-start(bf16[1024,1024]{1,0:T(8,128)(2,1)} %constant_dynamic-slice_fusion.4), channel_id=1, source_target_pairs={{0,2},{2,0},{4,6},{6,4},{8,10},{10,8},{12,14},{14,12},{16,18},{18,... | collective-permute-start | bytes 6291464 | tf_op jit(solution)/shard_map/ppermute | solution.py:400
  281.5 9.4 %copy-start.33 = (bf16[1024,2048]{1,0:T(8,128)(2,1)}, bf16[1024,2048]{1,0:T(8,128)(2,1)S(1)}, u32[]{:S(2)}) copy-start(bf16[1024,2048]{1,0:T(8,128)(2,1)S(1)} %constant_dynamic-update-slice_fusion.2) | copy-start | bytes 12582916
  291.1 9.7 %copy-start.32 = (bf16[2048,1024]{1,0:T(8,128)(2,1)}, bf16[2048,1024]{1,0:T(8,128)(2,1)S(1)}, u32[]{:S(2)}) copy-start(bf16[2048,1024]{1,0:T(8,128)(2,1)S(1)} %constant_dynamic-update-slice_fusion.4) | copy-start | bytes 12582916
  308.0 10.0 %copy-start.16 = (bf16[1024,2048]{1,0:T(8,128)(2,1)}, bf16[1024,2048]{1,0:T(8,128)(2,1)S(1)}, u32[]{:S(2)}) copy-start(bf16[1024,2048]{1,0:T(8,128)(2,1)S(1)} %convolution_convert_fusion) | copy-start | bytes 12582916
  309.5 85.0 %collective-permute-start.13 = (bf16[1024,1024]{1,0:T(8,128)(2,1)}, bf16[1024,1024]{1,0:T(8,128)(2,1)S(1)}, u32[]{:S(2)}, u32[]{:S(2)}) collective-permute-start(bf16[1024,1024]{1,0:T(8,128)(2,1)} %slice.193), channel_id=1, source_target_pairs={{0,2},{2,0},{4,6},{6,4},{8,10},{10,8},{12,14},{14,12},{16,18},{18,... | collective-permute-start | bytes 6291464 | tf_op jit(solution)/shard_map/ppermute | solution.py:400
  319.5 15.0 %collective-permute-start.10 = (bf16[1024,1024]{1,0:T(8,128)(2,1)}, bf16[1024,1024]{1,0:T(8,128)(2,1)S(1)}, u32[]{:S(2)}, u32[]{:S(2)}) collective-permute-start(bf16[1024,1024]{1,0:T(8,128)(2,1)} %slice.191), channel_id=1, source_target_pairs={{0,2},{2,0},{4,6},{6,4},{8,10},{10,8},{12,14},{14,12},{16,18},{18,... | collective-permute-start | bytes 6291464 | tf_op jit(solution)/shard_map/ppermute | solution.py:400
  334.3 6.3 collective-permute-start.16
  336.1 62.0 %collective-permute-start.11 = (bf16[1024,1024]{1,0:T(8,128)(2,1)}, bf16[1024,1024]{1,0:T(8,128)(2,1)}, u32[]{:S(2)}, u32[]{:S(2)}) collective-permute-start(bf16[1024,1024]{1,0:T(8,128)(2,1)} %slice_add_fusion.1), channel_id=1, source_target_pairs={{0,1},{1,0},{2,3},{3,2},{4,5},{5,4},{6,7},{7,6},{8,9},{9,8},{10,11... | collective-permute-start | bytes 6291464 | tf_op jit(solution)/shard_map/ppermute | solution.py:395
  337.6 6.9 collective-permute-start.15
  340.7 53.6 %collective-permute-start.17 = (bf16[256,1024]{1,0:T(8,128)(2,1)S(1)}, bf16[256,1024]{1,0:T(8,128)(2,1)S(1)}, u32[]{:S(2)}, u32[]{:S(2)}) collective-permute-start(bf16[256,1024]{1,0:T(8,128)(2,1)S(1)} %slice_add_fusion.3), channel_id=1, source_target_pairs={{0,1},{1,0},{2,3},{3,2},{4,5},{5,4},{6,7},{7,6},{8,9},{9,8},{10,11... | collective-permute-start | bytes 1572872 | tf_op jit(solution)/shard_map/ppermute | solution.py:395
  344.4 103.2 %collective-permute-start.12 = (bf16[1024,1024]{1,0:T(8,128)(2,1)}, bf16[1024,1024]{1,0:T(8,128)(2,1)}, u32[]{:S(2)}, u32[]{:S(2)}) collective-permute-start(bf16[1024,1024]{1,0:T(8,128)(2,1)} %constant_dynamic-slice_fusion.3), channel_id=1, source_target_pairs={{0,2},{2,0},{4,6},{6,4},{8,10},{10,8},{12,14},{14,12},{16,18},{18,... | collective-permute-start | bytes 6291464 | tf_op jit(solution)/shard_map/ppermute | solution.py:400
  394.6 150.5 %copy-start.2 = (bf16[256,1024]{1,0:T(8,128)(2,1)}, bf16[256,1024]{1,0:T(8,128)(2,1)S(1)}, u32[]{:S(2)}) copy-start(bf16[256,1024]{1,0:T(8,128)(2,1)S(1)} %add_add_fusion.8.others_1_) | copy-start | bytes 1572868
  397.9 49.7 %collective-permute-start.14 = (bf16[1024,1024]{1,0:T(8,128)(2,1)}, bf16[1024,1024]{1,0:T(8,128)(2,1)}, u32[]{:S(2)}, u32[]{:S(2)}) collective-permute-start(bf16[1024,1024]{1,0:T(8,128)(2,1)} %slice_add_fusion), channel_id=1, source_target_pairs={{0,1},{1,0},{2,3},{3,2},{4,5},{5,4},{6,7},{7,6},{8,9},{9,8},{10,11... | collective-permute-start | bytes 6291464 | tf_op jit(solution)/shard_map/ppermute | solution.py:395
  436.0 108.2 %all-reduce.5.cloned.1.call-start = ((), (), s32[]{:S(2)}) async-start(), calls=%async_computation | async-start | bytes 4194304 | tf_op jit(solution)/shard_map/psum | solution.py:426
  445.8 237.3 %collective-permute-start.18 = (bf16[3,1024,256]{2,1,0:T(8,128)(2,1)}, bf16[3,1024,256]{2,1,0:T(8,128)(2,1)}, u32[]{:S(2)}, u32[]{:S(2)}) collective-permute-start(bf16[3,1024,256]{2,1,0:T(8,128)(2,1)} %constant_dynamic-slice_fusion.1), channel_id=1, source_target_pairs={{0,2},{2,0},{4,6},{6,4},{8,10},{10,8},{12,14},{14,12},{16,18},{18,... | collective-permute-start | bytes 4718600 | tf_op jit(solution)/shard_map/ppermute | solution.py:400
  544.2 267.8 %collective-permute-start.24 = (bf16[1024,1024]{1,0:T(8,128)(2,1)}, bf16[1024,1024]{1,0:T(8,128)(2,1)}, u32[]{:S(2)}, u32[]{:S(2)}) collective-permute-start(bf16[1024,1024]{1,0:T(8,128)(2,1)} %all-reduce.5.cloned.1.call-done.others_2_), channel_id=1, source_target_pairs={{0,2},{2,0},{4,6},{6,4},{8,10},{10,8},{12,14},{14,12},{16,18},{18,... | collective-permute-start | bytes 6291464 | tf_op jit(solution)/shard_map/ppermute | solution.py:400
  577.7 105.3 %all-reduce.7.cloned.1.call-start = ((), (), s32[]{:S(2)}) async-start(), calls=%async_computation.1 | async-start | bytes 4194304 | tf_op jit(solution)/shard_map/psum | solution.py:426
  578.4 178.5 %all-reduce.9.cloned.1.call-start = ((), (), s32[]{:S(2)}) async-start(), calls=%async_computation.2 | async-start | bytes 1048576 | tf_op jit(solution)/shard_map/psum | solution.py:426
  584.8 8.7 copy-start.44
  584.8 11.0 %collective-permute-start.19 = (bf16[3,1024,256]{2,1,0:T(8,128)(2,1)S(1)}, bf16[3,1024,256]{2,1,0:T(8,128)(2,1)S(1)}, u32[]{:S(2)}, u32[]{:S(2)}) collective-permute-start(bf16[3,1024,256]{2,1,0:T(8,128)(2,1)S(1)} %slice.205), channel_id=1, source_target_pairs={{0,2},{2,0},{4,6},{6,4},{8,10},{10,8},{12,14},{14,12},{16,18},{18,... | collective-permute-start | bytes 4718600 | tf_op jit(solution)/shard_map/ppermute | solution.py:400
  597.1 86.1 %collective-permute-start.20 = (bf16[3,1024,256]{2,1,0:T(8,128)(2,1)}, bf16[3,1024,256]{2,1,0:T(8,128)(2,1)}, u32[]{:S(2)}, u32[]{:S(2)}) collective-permute-start(bf16[3,1024,256]{2,1,0:T(8,128)(2,1)} %slice_add_fusion.2), channel_id=1, source_target_pairs={{0,1},{1,0},{2,3},{3,2},{4,5},{5,4},{6,7},{7,6},{8,9},{9,8},{10,11... | collective-permute-start | bytes 4718600 | tf_op jit(solution)/shard_map/ppermute | solution.py:395
  616.2 143.3 %copy-start.45 = (f32[2048]{0:T(1024)S(1)}, f32[2048]{0:T(1024)}, u32[]{:S(2)}) copy-start(f32[2048]{0:T(1024)} %get-tuple-element.155) | copy-start | bytes 24580
  683.0 118.3 %copy-start.27 = (bf16[1024,1024]{0,1:T(8,128)(2,1)S(1)}, bf16[1024,1024]{0,1:T(8,128)(2,1)}, u32[]{:S(2)}) copy-start(bf16[1024,1024]{0,1:T(8,128)(2,1)} %get-tuple-element.115) | copy-start | bytes 6291460
  683.0 170.0 %all-reduce.11.cloned.1.call-start = ((), (), s32[]{:S(2)}) async-start(), calls=%async_computation.3 | async-start | bytes 3145728 | tf_op jit(solution)/shard_map/psum | solution.py:426
  757.0 105.5 %collective-permute-start.23 = (bf16[1024,1024]{1,0:T(8,128)(2,1)}, bf16[1024,1024]{1,0:T(8,128)(2,1)}, u32[]{:S(2)}, u32[]{:S(2)}) collective-permute-start(bf16[1024,1024]{1,0:T(8,128)(2,1)} %all-reduce.7.cloned.1.call-done), channel_id=1, source_target_pairs={{0,2},{2,0},{4,6},{6,4},{8,10},{10,8},{12,14},{14,12},{16,18},{18,... | collective-permute-start | bytes 6291464 | tf_op jit(solution)/shard_map/ppermute | solution.py:400
  811.1 48.5 %collective-permute-start.22 = (bf16[256,1024]{1,0:T(8,128)(2,1)S(1)}, bf16[256,1024]{1,0:T(8,128)(2,1)}, u32[]{:S(2)}, u32[]{:S(2)}) collective-permute-start(bf16[256,1024]{1,0:T(8,128)(2,1)S(1)} %copy-done.35), channel_id=1, source_target_pairs={{0,2},{2,0},{4,6},{6,4},{8,10},{10,8},{12,14},{14,12},{16,18},{18,... | collective-permute-start | bytes 1572872 | tf_op jit(solution)/shard_map/ppermute | solution.py:400
  853.0 16.0 %collective-permute-start.21 = (bf16[3,1024,256]{2,1,0:T(8,128)(2,1)}, bf16[3,1024,256]{2,1,0:T(8,128)(2,1)S(1)}, u32[]{:S(2)}, u32[]{:S(2)}) collective-permute-start(bf16[3,1024,256]{2,1,0:T(8,128)(2,1)} %all-reduce.11.cloned.1.call-done), channel_id=1, source_target_pairs={{0,2},{2,0},{4,6},{6,4},{8,10},{10,8},{12,14},{14,12},{16,18},{18,... | collective-permute-start | bytes 4718600 | tf_op jit(solution)/shard_map/ppermute | solution.py:400
  (41 other events, 135.3 us)
Sparse Core Ops, SparseCore 0:
  440.4 103.7 all-reduce.4
  582.1 100.8 all-reduce.6
  686.4 70.4 all-reduce.8
  761.3 91.6 all-reduce.10
